TPU v7x, 32 devices: a whole 2x2x4 slice. The times are simulated.
32 devices in a mesh: groups: 2 (over y), wide: 4 (over z), narrow: 2 (over x), sub: 2 (over core).
Axes of the slice: x: 2, y: 2, z: 4, core: 2. Of those that a mesh axis runs over, the one named last changes fastest.
Arguments:
- tokens: bfloat16 [128, 16384], P(('groups', 'wide'), ('narrow', 'sub')), parts along dimension 0, may hold values from -6 to 6
- gate_weight: bfloat16 [16384, 6656], P(('narrow', 'sub'), 'wide'), may hold values from -0.046875 to 0.046875
- up_weight: bfloat16 [16384, 6656], P(('narrow', 'sub'), 'wide'), may hold values from -0.046875 to 0.046875
- hidden_grad: bfloat16 [128, 6656], P(('groups', 'narrow', 'sub'), 'wide'), parts along dimension 0, may hold values from -6 to 6
Outputs:
- hidden: bfloat16 [128, 6656], P(('groups', 'narrow', 'sub'), 'wide'), parts along dimension 0
- input_grad: bfloat16 [128, 16384], P(('groups', 'wide'), ('narrow', 'sub')), parts along dimension 0
There are 2 independent parts, one for each index of `groups`. A program takes and returns all parts, laid end to end along the dimension named above; an argument that names none is the same for every part. Nothing has to cross between parts.
All inputs are finite; a program needn't handle non-finite values.
Results may differ from a plain program's by a relative error of at most 0.005.
Values may be sent and summed in bfloat16 or wider, within the bound.
No kernel may reach another device: no remote copies, remote signals or barrier semaphores. Data moves between devices by JAX's collectives and lax.ppermute only.
A program may use at most 128 MiB of HBM per device.

v0:
```python
import jax
import jax.numpy as jnp
from jax import lax
from jax.sharding import PartitionSpec as P


def times_transposed(left, right):
    return lax.dot_general(
        left, right, (((1,), (1,)), ((), ())), preferred_element_type=jnp.float32
    )


def activate(gate, up):
    sig = 1.0 / (1.0 + jnp.exp(-gate))
    act = gate * sig
    return (sig, act, (act * up).astype(jnp.bfloat16))


def backprop(grad_rows, gate, up, sig, act):
    grad = grad_rows.astype(jnp.float32)
    pre_gate = (grad * up * sig * (1.0 + gate * (1.0 - sig))).astype(jnp.bfloat16)
    pre_up = (grad * act).astype(jnp.bfloat16)
    return (pre_gate, pre_up)


def shards(tokens, gate_weight, up_weight, hidden_grad):
    hidden_cols = gate_weight.shape[1]
    all_rows = lax.all_gather(tokens, "wide", axis=0, tiled=True)
    joined = lax.psum_scatter(
        jnp.concatenate(
            [
                jnp.dot(all_rows, gate_weight, preferred_element_type=jnp.float32),
                jnp.dot(all_rows, up_weight, preferred_element_type=jnp.float32),
            ],
            axis=1,
        ),
        ("narrow", "sub"),
        scatter_dimension=0,
        tiled=True,
    )
    gate = joined[:, :hidden_cols]
    up = joined[:, hidden_cols:]
    sig, act, hidden = activate(gate, up)
    pre_gate, pre_up = backprop(hidden_grad, gate, up, sig, act)
    pre_gate_all, pre_up_all = (
        lax.all_gather(pre_gate, ("narrow", "sub"), axis=0, tiled=True),
        lax.all_gather(pre_up, ("narrow", "sub"), axis=0, tiled=True),
    )
    from_gate = lax.psum_scatter(
        times_transposed(pre_gate_all, gate_weight), "wide", scatter_dimension=0, tiled=True
    )
    from_up = lax.psum_scatter(
        times_transposed(pre_up_all, up_weight), "wide", scatter_dimension=0, tiled=True
    )
    input_grad = from_gate + from_up
    input_grad = input_grad.astype(jnp.bfloat16)
    return (hidden, input_grad)


def solution(mesh):
    return jax.shard_map(
        shards,
        mesh=mesh,
        in_specs=(
            P(("groups", "wide"), ("narrow", "sub")),
            P(("narrow", "sub"), "wide"),
            P(("narrow", "sub"), "wide"),
            P(("groups", "narrow", "sub"), "wide"),
        ),
        out_specs=(
            P(("groups", "narrow", "sub"), "wide"),
            P(("groups", "wide"), ("narrow", "sub")),
        ),
        check_vma=False,
    )
```

profile of v0, /device:TPU:0, one launch (start us, length us, event | category | flops | bytes accessed | tf_op | source)
XLA Modules:
  0.0 129.1 jit_solution(7139174299370568410)
XLA Ops:
  7.2 0.0 reduce-scatter.3.cloned.1.call-start
  7.2 0.0 copy-start
  7.2 17.7 %all_gather.9 = bf16[64,4096]{1,0:T(8,128)(2,1)S(1)} all-gather(bf16[16,4096]{1,0:T(8,128)(2,1)} %param.4), channel_id=1, replica_groups=mesh['groups'=2,'wide'=4,'narrow'=2,'sub'=2] {'wide'}, dimensions={0}, use_global_device_ids=true | all-gather | bytes 655360 | tf_op jit(solution)/shard_map/all_gather | solution.py:28
  24.9 7.3 %fusion.6 = f32[64,1664]{1,0:T(8,128)S(1)} fusion(bf16[64,4096]{1,0:T(8,128)(2,1)S(1)} %all_gather.9, bf16[4096,1664]{1,0:T(8,128)(2,1)} %param.6), kind=kOutput, calls=%fused_computation.12 | convolution fusion | flops 872415232 | bytes 14581760 | tf_op jit(solution)/shard_map/dot_general | solution.py:33
  32.2 0.0 copy-done
  32.2 0.0 copy-start.1
  32.2 2.4 %fusion.5 = f32[64,1664]{1,0:T(8,128)S(1)} fusion(bf16[64,4096]{1,0:T(8,128)(2,1)S(1)} %all_gather.9, bf16[4096,1664]{1,0:T(8,128)(2,1)S(1)} %copy-done), kind=kOutput, calls=%fused_computation.11 | convolution fusion | flops 872415232 | bytes 14581760 | tf_op jit(solution)/shard_map/dot_general | solution.py:32
  34.6 1.0 pad_maximum_fusion
  35.6 0.0 reduce-scatter.3.cloned.1.call-update
  35.6 0.0 reduce-scatter.5.cloned.1.call-start
  35.7 25.5 %reduce-scatter.3.cloned.1.call-done = f32[16,3328]{1,0:T(8,128)} async-done(((f32[64,3328]{1,0:T(8,128)}), f32[16,3328]{1,0:T(8,128)}) %reduce-scatter.3.cloned.1.call-update) | async-done | bytes 213008 | tf_op jit(solution)/shard_map/reduce_scatter | solution.py:29
  61.2 0.0 copy-done.1
  61.2 1.6 %fusion.3 = (bf16[16,1664]{1,0:T(8,128)(2,1)S(1)}, bf16[16,1664]{1,0:T(8,128)(2,1)S(1)}, bf16[16,1664]{1,0:T(8,128)(2,1)}) fusion(bf16[16,1664]{1,0:T(8,128)(2,1)S(1)} %copy-done.1, f32[16,3328]{1,0:T(8,128)} %reduce-scatter.3.cloned.1.call-done), kind=kLoop, calls=%fused_computation.7 | loop fusion | flops 425984 | bytes 425984 | tf_op jit(solution)/shard_map/convert_element_type | solution.py:22
  62.8 5.6 %all_gather.11 = bf16[64,1664]{1,0:T(8,128)(2,1)S(1)} all-gather(bf16[16,1664]{1,0:T(8,128)(2,1)S(1)} %get-tuple-element.2), channel_id=1, replica_groups=mesh['groups'=2,'wide'=4,'narrow'=2,'sub'=2] {'narrow','sub'}, dimensions={0}, use_global_device_ids=true | all-gather | bytes 266240 | tf_op jit(solution)/shard_map/all_gather | solution.py:47
  68.5 5.6 %all_gather.10 = bf16[64,1664]{1,0:T(8,128)(2,1)S(1)} all-gather(bf16[16,1664]{1,0:T(8,128)(2,1)S(1)} %get-tuple-element.3), channel_id=1, replica_groups=mesh['groups'=2,'wide'=4,'narrow'=2,'sub'=2] {'narrow','sub'}, dimensions={0}, use_global_device_ids=true | all-gather | bytes 266240 | tf_op jit(solution)/shard_map/all_gather | solution.py:46
  74.1 9.1 %fusion.7 = f32[64,4096]{1,0:T(8,128)S(1)} fusion(bf16[64,1664]{1,0:T(8,128)(2,1)S(1)} %all_gather.10, bf16[4096,1664]{1,0:T(8,128)(2,1)} %param.5), kind=kOutput, calls=%fused_computation.13 | convolution fusion | flops 872415232 | bytes 14893056 | tf_op jit(solution)/shard_map/dot_general | solution.py:8
  83.2 10.1 %convolution_add_fusion = f32[64,4096]{1,0:T(8,128)} fusion(f32[64,4096]{1,0:T(8,128)S(1)} %fusion.7, bf16[64,1664]{1,0:T(8,128)(2,1)S(1)} %all_gather.11, bf16[4096,1664]{1,0:T(8,128)(2,1)} %param.6), kind=kOutput, calls=%fused_computation | convolution fusion | flops 872677376 | bytes 15941632 | tf_op jit(solution)/shard_map/dot_general | solution.py:8
  93.3 0.0 reduce-scatter.5.cloned.1.call-update
  93.3 27.3 %reduce-scatter.5.cloned.1.call-done = f32[16,4096]{1,0:T(8,128)} async-done(((f32[64,4096]{1,0:T(8,128)}), f32[16,4096]{1,0:T(8,128)}) %reduce-scatter.5.cloned.1.call-update) | async-done | bytes 262160 | tf_op jit(solution)/shard_map/reduce_scatter | solution.py:49
  120.7 1.6 %convert_element_type.19 = bf16[16,4096]{1,0:T(8,128)(2,1)} convert(f32[16,4096]{1,0:T(8,128)} %reduce-scatter.5.cloned.1.call-done) | non-fusion elementwise | flops 65536 | bytes 393216 | tf_op jit(solution)/shard_map/convert_element_type | solution.py:56
Async XLA Ops:
  7.2 54.0 %reduce-scatter.3.cloned.1.call-start = ((), (), s32[]{:S(2)}) async-start(), calls=%async_computation.2 | async-start | bytes 1064960 | tf_op jit(solution)/shard_map/reduce_scatter | solution.py:29
  7.2 25.0 %copy-start = (bf16[4096,1664]{1,0:T(8,128)(2,1)S(1)}, bf16[4096,1664]{1,0:T(8,128)(2,1)}, u32[]{:S(2)}) copy-start(bf16[4096,1664]{1,0:T(8,128)(2,1)} %param.5) | copy-start | bytes 40894468
  32.2 29.0 %copy-start.1 = (bf16[16,1664]{1,0:T(8,128)(2,1)S(1)}, bf16[16,1664]{1,0:T(8,128)(2,1)}, u32[]{:S(2)}) copy-start(bf16[16,1664]{1,0:T(8,128)(2,1)} %param.7) | copy-start | bytes 159748
  35.6 85.0 %reduce-scatter.5.cloned.1.call-start = ((), (), s32[]{:S(2)}) async-start(), calls=%async_computation.3 | async-start | bytes 1310720 | tf_op jit(solution)/shard_map/reduce_scatter | solution.py:49
Sparse Core Ops, SparseCore 0:
  35.8 25.3 reduce-scatter.2
  93.4 27.1 reduce-scatter.4
where the time goes:
time: 129 us
  waiting for transfers between devices  52.9 us (41%)
  blocking collectives  29 us (22%)
  matrix products  28.9 us (22%)
  between operations  14.1 us (11%)
  other arithmetic  4.21 us (3%)
    reduce_scatter x1, waiting for transfers between devices, shards(): lax.psum_scatter(times_transposed(pre_gate_all, gate_weight), 'wide', sca...  27.3 us
    reduce_scatter x1, waiting for transfers between devices, shards(): lax.psum_scatter(jnp.concatenate([jnp.dot(all_rows, gate_weight, preferre...  25.5 us
    dot_general x2, matrix products, times_transposed(): lax.dot_general(left, right, (((1,), (1,)), ((), ())), preferred_element_...  19.2 us
    all_gather x1, blocking collectives, shards(): all_rows = lax.all_gather(tokens, 'wide', axis=0, tiled=True)  17.7 us
    dot_general x1, matrix products, shards(): jnp.dot(all_rows, up_weight, preferred_element_type=jnp.float32)  7.28 us
    all_gather x1, blocking collectives, shards(): lax.all_gather(pre_up, ('narrow', 'sub'), axis=0, tiled=True)  5.64 us
    all_gather x1, blocking collectives, shards(): lax.all_gather(pre_gate, ('narrow', 'sub'), axis=0, tiled=True)  5.64 us
  transfers between devices with their start and end apart: 2, of which 2 were waited for; matrix products, arithmetic and copies ran while one was open for 0% of the time, Pallas kernels for 0%

commit v1 on v0

v1 whole, which is shorter than its diff:
```python
import functools
import math

import jax
import jax.numpy as jnp
from jax import lax
from jax.experimental import pallas as pl
from jax.experimental.pallas import tpu as pltpu
from jax.sharding import PartitionSpec as P

VMEM = pl.BlockSpec(memory_space=pltpu.VMEM)
PARAMS = pltpu.CompilerParams(vmem_limit_bytes=8 << 20)
NT = (((1,), (1,)), ((), ()))


def partner(index, step, size):
    return index ^ step if size & (size - 1) == 0 else (index + step) % size


def source(index, step, size):
    return index ^ step if size & (size - 1) == 0 else (index + size - step) % size


def exchange(x, axis, step, size):
    return lax.ppermute(x, axis, [(i, partner(i, step, size)) for i in range(size)])


def tiles(width, tile=256):
    return width // tile, width // tile * tile


def load_weights(gate_weight, up_weight, parts=4):
    rows = gate_weight.shape[0]
    step = rows // parts

    def kernel(gate_hbm, up_hbm, gate_out, up_out, sems):
        copies = []
        for i in range(parts):
            span = pl.ds(i * step, step)
            copies.append(pltpu.make_async_copy(gate_hbm.at[span], gate_out.at[span], sems.at[2 * i]))
            copies.append(pltpu.make_async_copy(up_hbm.at[span], up_out.at[span], sems.at[2 * i + 1]))
        for copy in copies:
            copy.start()
        for copy in copies:
            copy.wait()

    shape = gate_weight.shape
    return pl.pallas_call(
        kernel,
        out_shape=[pltpu.VMEM(shape, jnp.bfloat16)] * 2,
        in_specs=[pl.BlockSpec(memory_space=pltpu.HBM)] * 2,
        out_specs=[VMEM] * 2,
        scratch_shapes=[pltpu.SemaphoreType.DMA((2 * parts,))],
        compiler_params=PARAMS,
        cost_estimate=pl.CostEstimate(flops=0, bytes_accessed=2 * 2 * gate_weight.size, transcendentals=0),
        name="load_weights",
    )(gate_weight, up_weight)


def forward(blocks, gate_weight, up_weight, sizes):
    wide, narrow, sub = sizes
    block_rows, depth = blocks[0].shape
    hidden_cols = gate_weight.shape[1]
    rows = block_rows * wide
    share = rows // (narrow * sub)
    piece = math.gcd(block_rows, share)
    half = rows // sub

    def kernel(*refs):
        block_refs = refs[:wide]
        gate_ref, up_ref, keep_ref, send_ref, x_ref = refs[wide:]
        me, core = lax.axis_index("wide"), lax.axis_index("sub")
        for step, block in enumerate(block_refs):
            owner = source(me, step, wide)
            for i in range(block_rows // piece):
                row = owner * block_rows + i * piece
                part = row // share
                place = ((part % sub) ^ core) * half + part // sub * share + row % share
                x_ref[pl.ds(pl.multiple_of(place, piece), piece), :] = block[pl.ds(i * piece, piece), :]

        def columns(weight, start, width, out):
            product = jnp.dot(x_ref[...], weight[:, pl.ds(start, width)], preferred_element_type=jnp.float32)
            keep_ref[:, pl.ds(out, width)] = product[:half]
            send_ref[:, pl.ds(out, width)] = product[half:]

        whole, rest = tiles(hidden_cols)
        for i, weight in enumerate((gate_ref, up_ref)):

            def body(t, carry, i=i, weight=weight):
                start = pl.multiple_of(t * 256, 256)
                columns(weight, start, 256, pl.multiple_of(start + i * hidden_cols, 128))
                return carry

            lax.fori_loop(0, whole, body, 0)
            if rest < hidden_cols:
                columns(weight, rest, hidden_cols - rest, rest + i * hidden_cols)

    shape = jax.ShapeDtypeStruct((half, 2 * hidden_cols), jnp.float32)
    return pl.pallas_call(
        kernel,
        out_shape=[shape] * 2,
        in_specs=[VMEM] * (wide + 2),
        out_specs=[VMEM] * 2,
        scratch_shapes=[pltpu.VMEM((rows, depth), jnp.bfloat16)],
        compiler_params=PARAMS,
        name="forward",
    )(*blocks, gate_weight, up_weight)


def activate(own, others, grads, sizes):
    wide, narrow, sub = sizes
    rows, both = own.shape
    hidden_cols = both // 2
    share = rows // narrow

    def kernel(*refs):
        own_ref = refs[0]
        other_refs = refs[1:narrow]
        grad_refs = refs[narrow : 2 * narrow]
        hidden_ref, pre_ref = refs[2 * narrow :]
        me = lax.axis_index("narrow")
        for step, grad_ref in enumerate(grad_refs):
            row = pl.ds(pl.multiple_of(source(me, step, narrow) * share, share), share)

            def total(cols, row=row):
                value = own_ref[row, cols]
                for other in other_refs:
                    value += other[row, cols].astype(jnp.float32)
                return value

            for start in range(0, hidden_cols, 128):
                cols = pl.ds(start, 128)
                up_cols = pl.ds(start + hidden_cols, 128)
                gate, up = total(cols), total(up_cols)
                sig = 1.0 / (1.0 + jnp.exp(-gate))
                act = gate * sig
                if step == 0:
                    hidden_ref[:, cols] = (act * up).astype(jnp.bfloat16)
                grad = grad_ref[:, cols].astype(jnp.float32)
                pre_ref[row, cols] = (grad * up * sig * (1.0 + gate * (1.0 - sig))).astype(jnp.bfloat16)
                pre_ref[row, up_cols] = (grad * act).astype(jnp.bfloat16)

    return pl.pallas_call(
        kernel,
        out_shape=[
            jax.ShapeDtypeStruct((share, hidden_cols), jnp.bfloat16),
            jax.ShapeDtypeStruct((rows, both), jnp.bfloat16),
        ],
        in_specs=[VMEM] * (2 * narrow),
        out_specs=[VMEM] * 2,
        compiler_params=PARAMS,
        name="activate",
    )(own, *others, *grads)


def backward(own, other, gate_weight, up_weight, sizes):
    wide, narrow, sub = sizes
    half, both = own.shape
    hidden_cols = both // 2
    rows = half * sub
    block_rows = rows // wide
    share = half // narrow
    piece = math.gcd(block_rows, share)
    depth = gate_weight.shape[0]

    def kernel(own_ref, other_ref, gate_ref, up_ref, *refs):
        out_refs, pre_ref = refs[:wide], refs[wide]
        me, core = lax.axis_index("wide"), lax.axis_index("sub")
        for flip, ref in enumerate((own_ref, other_ref)):
            for i in range(half // piece):
                row = (i * piece // share * sub + (core ^ flip)) * share + i * piece % share
                place = source(row // block_rows, me, wide) * block_rows + row % block_rows
                pre_ref[pl.ds(pl.multiple_of(place, piece), piece), :] = ref[pl.ds(i * piece, piece), :]

        def body(t, carry):
            cols = pl.ds(pl.multiple_of(t * 256, 256), 256)
            product = lax.dot_general(
                pre_ref[:, :hidden_cols], gate_ref[cols, :], NT, preferred_element_type=jnp.float32
            )
            product += lax.dot_general(
                pre_ref[:, hidden_cols:], up_ref[cols, :], NT, preferred_element_type=jnp.float32
            )
            for step, out in enumerate(out_refs):
                out[:, cols] = product[step * block_rows : (step + 1) * block_rows].astype(out.dtype)
            return carry

        lax.fori_loop(0, depth // 256, body, 0)

    return pl.pallas_call(
        kernel,
        out_shape=[
            jax.ShapeDtypeStruct((block_rows, depth), jnp.bfloat16 if step else jnp.float32)
            for step in range(wide)
        ],
        in_specs=[VMEM] * 4,
        out_specs=[VMEM] * wide,
        scratch_shapes=[pltpu.VMEM((rows, both), jnp.bfloat16)],
        compiler_params=PARAMS,
        name="backward",
    )(own, other, gate_weight, up_weight)


def shards(tokens, gate_weight, up_weight, hidden_grad, sizes):
    wide, narrow, sub = sizes
    order = [2, 3, 1] if wide == 4 else range(1, wide)
    got = {step: exchange(tokens, "wide", step, wide) for step in order}
    blocks = [tokens] + [got[step] for step in range(1, wide)]
    grads = [hidden_grad] + [exchange(hidden_grad, "narrow", step, narrow) for step in range(1, narrow)]
    gate_weight, up_weight = load_weights(gate_weight, up_weight)
    keep, send = forward(blocks, gate_weight, up_weight, sizes)
    chip = keep + exchange(send, "sub", 1, sub)
    chip_bf16 = chip.astype(jnp.bfloat16)
    others = [exchange(chip_bf16, "narrow", step, narrow) for step in range(1, narrow)]
    hidden, pre = activate(chip, others, grads, sizes)
    pre_other = exchange(pre, "sub", 1, sub)
    own, *sends = backward(pre, pre_other, gate_weight, up_weight, sizes)
    got = {step: exchange(sends[step - 1], "wide", step, wide) for step in order}
    input_grad = own
    for step in range(1, wide):
        input_grad = input_grad + got[step].astype(jnp.float32)
    return (hidden, input_grad.astype(jnp.bfloat16))


def solution(mesh):
    sizes = tuple(mesh.shape[axis] for axis in ("wide", "narrow", "sub"))
    return jax.shard_map(
        functools.partial(shards, sizes=sizes),
        mesh=mesh,
        in_specs=(
            P(("groups", "wide"), ("narrow", "sub")),
            P(("narrow", "sub"), "wide"),
            P(("narrow", "sub"), "wide"),
            P(("groups", "narrow", "sub"), "wide"),
        ),
        out_specs=(
            P(("groups", "narrow", "sub"), "wide"),
            P(("groups", "wide"), ("narrow", "sub")),
        ),
        check_vma=False,
    )
```

time: 129 us -> 62 us (0.48)
  waiting for transfers between devices: 52.9 us -> 20.3 us
  blocking collectives: 29 us -> 0 us
  matrix products: 28.9 us -> 0 us
  Pallas kernels: 0 us -> 22.9 us
  between operations: 14.1 us -> 0.69 us
  starting transfers between devices: 0.08 us -> 12.3 us
  local copies, waits for them, and re-layouts: 0.01 us -> 4.88 us
  other arithmetic: 4.21 us -> 0.78 us
    reduce_scatter x2 -> x0, waiting for transfers between devices: 52.9 us -> none  [the longest x1 27.3 us: shards(): lax.psum_scatter(times_transposed(pre_gate_all, gate_weight), 'wide', sca...]
    all_gather x3 -> x0, blocking collectives: 29 us -> none  [the longest x1 17.7 us: shards(): all_rows = lax.all_gather(tokens, 'wide', axis=0, tiled=True)]
    dot_general x4 -> x0, matrix products: 28.9 us -> none  [the longest x2 19.2 us: times_transposed(): lax.dot_general(left, right, (((1,), (1,)), ((), ())), preferred_element_...]
    pallas_call x0 -> x4, Pallas kernels: none -> 22.9 us  [the longest x1 10.2 us: backward(): pl.pallas_call(kernel, out_shape=[jax.ShapeDtypeStruct((block_rows, depth...]
    ppermute x0 -> x10, waiting for transfers between devices: none -> 20.3 us  [exchange(): lax.ppermute(x, axis, [(i, partner(i, step, size)) for i in range(size)])]
    ppermute x0 -> x10, starting transfers between devices: none -> 12.3 us  [exchange(): lax.ppermute(x, axis, [(i, partner(i, step, size)) for i in range(size)])]
    unnamed x4 -> x6, local copies, waits for them, and re-layouts: 0.01 us -> 4.88 us
    convert_element_type x2, other arithmetic: 3.25 us -> 0.78 us  [the longest x1 0.72 us: shards(): return (hidden, input_grad.astype(jnp.bfloat16))]
  transfers between devices with their start and end apart: 2 -> 10, of which waited for: 2 -> 6; matrix products, arithmetic and copies ran while one was open for 0% -> 0% of each run, Pallas kernels for 0% -> 9%
where the time goes in v1:
time: 62 us; the launch traced here: 61.9 us
  Pallas kernels  22.9 us (37%)
  waiting for transfers between devices  20.3 us (33%)
  starting transfers between devices  12.3 us (20%)
  local copies, waits for them, and re-layouts  4.88 us (8%)
  other arithmetic  0.78 us (1%)
  between operations  0.69 us (1%)
    ppermute x10, waiting for transfers between devices, exchange(): lax.ppermute(x, axis, [(i, partner(i, step, size)) for i in range(size)])  20.3 us
    ppermute x10, starting transfers between devices, exchange(): lax.ppermute(x, axis, [(i, partner(i, step, size)) for i in range(size)])  12.3 us
    pallas_call x1, Pallas kernels, backward(): pl.pallas_call(kernel, out_shape=[jax.ShapeDtypeStruct((block_rows, depth...  10.2 us
    pallas_call x1, Pallas kernels, forward(): pl.pallas_call(kernel, out_shape=[shape] * 2, in_specs=[VMEM] * (wide + 2...  6.53 us
    pallas_call x1, Pallas kernels, load_weights(): pl.pallas_call(kernel, out_shape=[pltpu.VMEM(shape, jnp.bfloat16)] * 2, i...  5.41 us
    unnamed x6, local copies, waits for them, and re-layouts  4.88 us
  transfers between devices with their start and end apart: 10, of which 6 were waited for; matrix products, arithmetic and copies ran while one was open for 0% of the time, Pallas kernels for 9%

profile of v1, /device:TPU:0, one launch (start us, length us, event | category | flops | bytes accessed | tf_op | source)
XLA Modules:
  0.0 61.9 jit_solution(12644767628817525931)
XLA Ops:
  0.6 3.1 %collective-permute-start = (bf16[16,4096]{1,0:T(8,128)(2,1)}, bf16[16,4096]{1,0:T(8,128)(2,1)S(1)}, u32[]{:S(2)}, u32[]{:S(2)}) collective-permute-start(bf16[16,4096]{1,0:T(8,128)(2,1)} %refs_0_.1), channel_id=1, source_target_pairs={{0,4},{4,0},{8,12},{12,8},{1,5},{5,1},{9,13},{13,9},{2,6},{6,2},{1... | collective-permute-start | bytes 393224 | tf_op jit(solution)/shard_map/ppermute | solution.py:25
  3.7 2.6 %collective-permute-start.1 = (bf16[16,4096]{1,0:T(8,128)(2,1)}, bf16[16,4096]{1,0:T(8,128)(2,1)S(1)}, u32[]{:S(2)}, u32[]{:S(2)}) collective-permute-start(bf16[16,4096]{1,0:T(8,128)(2,1)} %refs_0_.1), channel_id=1, source_target_pairs={{0,8},{4,12},{8,0},{12,4},{1,9},{5,13},{9,1},{13,5},{2,10},{6,14},... | collective-permute-start | bytes 393224 | tf_op jit(solution)/shard_map/ppermute | solution.py:25
  6.3 0.0 collective-permute-start.2
  6.3 0.0 copy-start
  6.3 4.9 %copy-done = bf16[4096,1664]{1,0:T(8,128)(2,1)S(1)} copy-done((bf16[4096,1664]{1,0:T(8,128)(2,1)S(1)}, bf16[4096,1664]{1,0:T(8,128)(2,1)}, u32[]{:S(2)}) %copy-start) | copy-done | bytes 13631512
  11.2 0.0 copy-start.1
  11.2 5.4 %load_weights.1 = (bf16[4096,1664]{1,0:T(8,128)(2,1)S(1)}, bf16[4096,1664]{1,0:T(8,128)(2,1)S(1)}) custom-call(bf16[4096,1664]{1,0:T(8,128)(2,1)S(1)} %copy-done, bf16[4096,1664]{1,0:T(8,128)(2,1)} %up_hbm.1), custom_call_target="tpu_custom_call" | custom-call | bytes 27262976 | tf_op jit(solution)/shard_map/load_weights/pallas_call | solution.py:48
  16.6 0.0 collective-permute-done.refs_1_
  16.6 0.3 collective-permute-done.1.refs_2_
  16.9 0.0 collective-permute-done.2.refs_3_
  16.9 0.0 copy-done.1
  16.9 0.0 copy-start.2
  16.9 6.5 %forward.1 = (f32[32,3328]{1,0:T(8,128)S(1)}, f32[32,3328]{1,0:T(8,128)S(1)}) custom-call(bf16[16,4096]{1,0:T(8,128)(2,1)S(1)} %copy-done.1, bf16[16,4096]{1,0:T(8,128)(2,1)S(1)} %collective-permute-done.refs_1_, bf16[16,4096]{1,0:T(8,128)(2,1)S(1)} %collective-permute-done.1.refs_2_, bf16[16,4096]{1,0:T(8,128)(2,1)S(1)} %collective-permute-done.2.refs_3_, ...), custom_call_target="tpu_custom_call" | custom-call | tf_op jit(solution)/shard_map/forward/pallas_call | solution.py:99
  23.4 0.1 collective-permute-start.3
  23.5 1.8 %collective-permute-done.3 = f32[32,3328]{1,0:T(8,128)S(1)} collective-permute-done((f32[32,3328]{1,0:T(8,128)S(1)}, f32[32,3328]{1,0:T(8,128)S(1)}, u32[]{:S(2)}, u32[]{:S(2)}) %collective-permute-start.3) | collective-permute-done | bytes 426016 | tf_op jit(solution)/shard_map/ppermute | solution.py:25
  25.3 0.1 fusion
  25.3 1.6 %collective-permute-start.4 = (bf16[32,3328]{1,0:T(8,128)(2,1)S(1)}, bf16[32,3328]{1,0:T(8,128)(2,1)S(1)}, u32[]{:S(2)}, u32[]{:S(2)}) collective-permute-start(bf16[32,3328]{1,0:T(8,128)(2,1)S(1)} %get-tuple-element.22), channel_id=1, source_target_pairs={{0,2},{2,0},{1,3},{3,1},{4,6},{6,4},{5,7},{7,5},{8,10},{10,8},{9,1... | collective-permute-start | bytes 638984 | tf_op jit(solution)/shard_map/ppermute | solution.py:25
  26.9 0.0 copy-done.2
  26.9 0.5 collective-permute-start.5
  27.4 6.4 %collective-permute-done.5.refs_3_ = bf16[16,1664]{1,0:T(8,128)(2,1)S(1)} collective-permute-done((bf16[16,1664]{1,0:T(8,128)(2,1)S(1)}, bf16[16,1664]{1,0:T(8,128)(2,1)S(1)}, u32[]{:S(2)}, u32[]{:S(2)}) %collective-permute-start.5) | collective-permute-done | bytes 53280 | tf_op jit(solution)/shard_map/ppermute | solution.py:25
  33.8 0.0 collective-permute-done.4.refs_1_
  33.8 0.7 %activate.1 = (bf16[16,1664]{1,0:T(8,128)(2,1)}, bf16[32,3328]{1,0:T(8,128)(2,1)S(1)}) custom-call(f32[32,3328]{1,0:T(8,128)S(1)} %get-tuple-element.23.refs_0_, bf16[32,3328]{1,0:T(8,128)(2,1)S(1)} %collective-permute-done.4.refs_1_, bf16[16,1664]{1,0:T(8,128)(2,1)S(1)} %copy-done.2, bf16[16,1664]{1,0:T(8,128)(2,1)S(1)} %collective-permute-done.5.refs_3_), custom_call_target="tpu_custom_call" | custom-call | tf_op jit(solution)/shard_map/activate/pallas_call | solution.py:143
  34.5 0.0 collective-permute-start.6
  34.5 1.5 %collective-permute-done.6.other_ref = bf16[32,3328]{1,0:T(8,128)(2,1)S(1)} collective-permute-done((bf16[32,3328]{1,0:T(8,128)(2,1)S(1)}, bf16[32,3328]{1,0:T(8,128)(2,1)S(1)}, u32[]{:S(2)}, u32[]{:S(2)}) %collective-permute-start.6) | collective-permute-done | bytes 213024 | tf_op jit(solution)/shard_map/ppermute | solution.py:25
  36.0 10.2 %backward.1 = (f32[16,4096]{1,0:T(8,128)S(1)}, bf16[16,4096]{1,0:T(8,128)(2,1)S(1)}, bf16[16,4096]{1,0:T(8,128)(2,1)S(1)}, bf16[16,4096]{1,0:T(8,128)(2,1)S(1)}) custom-call(bf16[32,3328]{1,0:T(8,128)(2,1)S(1)} %get-tuple-element.17.own_ref, bf16[32,3328]{1,0:T(8,128)(2,1)S(1)} %collective-permute-done.6.other_ref, ...), custom_call_target="tpu_custom_call" | custom-call | tf_op jit(solution)/shard_map/backward/pallas_call | solution.py:189
  46.2 2.0 %collective-permute-start.7 = (bf16[16,4096]{1,0:T(8,128)(2,1)S(1)}, bf16[16,4096]{1,0:T(8,128)(2,1)S(1)}, u32[]{:S(2)}, u32[]{:S(2)}) collective-permute-start(bf16[16,4096]{1,0:T(8,128)(2,1)S(1)} %get-tuple-element.19), channel_id=1, source_target_pairs={{0,4},{4,0},{8,12},{12,8},{1,5},{5,1},{9,13},{13,9},{2,6},{6,2},{1... | collective-permute-start | bytes 393224 | tf_op jit(solution)/shard_map/ppermute | solution.py:25
  48.3 2.2 %collective-permute-start.8 = (bf16[16,4096]{1,0:T(8,128)(2,1)S(1)}, bf16[16,4096]{1,0:T(8,128)(2,1)S(1)}, u32[]{:S(2)}, u32[]{:S(2)}) collective-permute-start(bf16[16,4096]{1,0:T(8,128)(2,1)S(1)} %get-tuple-element.20), channel_id=1, source_target_pairs={{0,8},{4,12},{8,0},{12,4},{1,9},{5,13},{9,1},{13,5},{2,10},{6,14},... | collective-permute-start | bytes 393224 | tf_op jit(solution)/shard_map/ppermute | solution.py:25
  50.5 0.3 collective-permute-start.9
  50.7 3.2 %collective-permute-done.7 = bf16[16,4096]{1,0:T(8,128)(2,1)S(1)} collective-permute-done((bf16[16,4096]{1,0:T(8,128)(2,1)S(1)}, bf16[16,4096]{1,0:T(8,128)(2,1)S(1)}, u32[]{:S(2)}, u32[]{:S(2)}) %collective-permute-start.7) | collective-permute-done | bytes 131104 | tf_op jit(solution)/shard_map/ppermute | solution.py:25
  53.9 7.2 %collective-permute-done.8 = bf16[16,4096]{1,0:T(8,128)(2,1)S(1)} collective-permute-done((bf16[16,4096]{1,0:T(8,128)(2,1)S(1)}, bf16[16,4096]{1,0:T(8,128)(2,1)S(1)}, u32[]{:S(2)}, u32[]{:S(2)}) %collective-permute-start.8) | collective-permute-done | bytes 131104 | tf_op jit(solution)/shard_map/ppermute | solution.py:25
  61.2 0.0 collective-permute-done.9
  61.2 0.7 %add_convert_fusion = bf16[16,4096]{1,0:T(8,128)(2,1)} fusion(bf16[16,4096]{1,0:T(8,128)(2,1)S(1)} %collective-permute-done.9, bf16[16,4096]{1,0:T(8,128)(2,1)S(1)} %collective-permute-done.8, f32[16,4096]{1,0:T(8,128)S(1)} %get-tuple-element.18, bf16[16,4096]{1,0:T(8,128)(2,1)S(1)} %collective-permute-done.7), kind=kLoop, calls=%fused_computation | loop fusion | flops 458752 | bytes 786432 | tf_op jit(solution)/shard_map/convert_element_type | solution.py:221
Async XLA Ops:
  0.6 16.0 %collective-permute-start = (bf16[16,4096]{1,0:T(8,128)(2,1)}, bf16[16,4096]{1,0:T(8,128)(2,1)S(1)}, u32[]{:S(2)}, u32[]{:S(2)}) collective-permute-start(bf16[16,4096]{1,0:T(8,128)(2,1)} %refs_0_.1), channel_id=1, source_target_pairs={{0,4},{4,0},{8,12},{12,8},{1,5},{5,1},{9,13},{13,9},{2,6},{6,2},{1... | collective-permute-start | bytes 393224 | tf_op jit(solution)/shard_map/ppermute | solution.py:25
  3.7 13.2 %collective-permute-start.1 = (bf16[16,4096]{1,0:T(8,128)(2,1)}, bf16[16,4096]{1,0:T(8,128)(2,1)S(1)}, u32[]{:S(2)}, u32[]{:S(2)}) collective-permute-start(bf16[16,4096]{1,0:T(8,128)(2,1)} %refs_0_.1), channel_id=1, source_target_pairs={{0,8},{4,12},{8,0},{12,4},{1,9},{5,13},{9,1},{13,5},{2,10},{6,14},... | collective-permute-start | bytes 393224 | tf_op jit(solution)/shard_map/ppermute | solution.py:25
  6.3 10.6 %collective-permute-start.2 = (bf16[16,4096]{1,0:T(8,128)(2,1)}, bf16[16,4096]{1,0:T(8,128)(2,1)S(1)}, u32[]{:S(2)}, u32[]{:S(2)}) collective-permute-start(bf16[16,4096]{1,0:T(8,128)(2,1)} %refs_0_.1), channel_id=1, source_target_pairs={{0,12},{4,8},{8,4},{12,0},{1,13},{5,9},{9,5},{13,1},{2,14},{6,10},... | collective-permute-start | bytes 393224 | tf_op jit(solution)/shard_map/ppermute | solution.py:25
  6.3 4.9 %copy-start = (bf16[4096,1664]{1,0:T(8,128)(2,1)S(1)}, bf16[4096,1664]{1,0:T(8,128)(2,1)}, u32[]{:S(2)}) copy-start(bf16[4096,1664]{1,0:T(8,128)(2,1)} %gate_hbm.1) | copy-start | bytes 40894468
  11.2 5.7 %copy-start.1 = (bf16[16,4096]{1,0:T(8,128)(2,1)S(1)}, bf16[16,4096]{1,0:T(8,128)(2,1)}, u32[]{:S(2)}) copy-start(bf16[16,4096]{1,0:T(8,128)(2,1)} %refs_0_.1) | copy-start | bytes 393220
  16.9 10.0 %copy-start.2 = (bf16[16,1664]{1,0:T(8,128)(2,1)S(1)}, bf16[16,1664]{1,0:T(8,128)(2,1)}, u32[]{:S(2)}) copy-start(bf16[16,1664]{1,0:T(8,128)(2,1)} %refs_2_.1) | copy-start | bytes 159748
  23.4 1.8 %collective-permute-start.3 = (f32[32,3328]{1,0:T(8,128)S(1)}, f32[32,3328]{1,0:T(8,128)S(1)}, u32[]{:S(2)}, u32[]{:S(2)}) collective-permute-start(f32[32,3328]{1,0:T(8,128)S(1)} %get-tuple-element.15), channel_id=1, source_target_pairs={{0,1},{1,0},{2,3},{3,2},{4,5},{5,4},{6,7},{7,6},{8,9},{9,8},{10,11... | collective-permute-start | bytes 1277960 | tf_op jit(solution)/shard_map/ppermute | solution.py:25
  25.3 8.5 %collective-permute-start.4 = (bf16[32,3328]{1,0:T(8,128)(2,1)S(1)}, bf16[32,3328]{1,0:T(8,128)(2,1)S(1)}, u32[]{:S(2)}, u32[]{:S(2)}) collective-permute-start(bf16[32,3328]{1,0:T(8,128)(2,1)S(1)} %get-tuple-element.22), channel_id=1, source_target_pairs={{0,2},{2,0},{1,3},{3,1},{4,6},{6,4},{5,7},{7,5},{8,10},{10,8},{9,1... | collective-permute-start | bytes 638984 | tf_op jit(solution)/shard_map/ppermute | solution.py:25
  26.9 6.9 %collective-permute-start.5 = (bf16[16,1664]{1,0:T(8,128)(2,1)S(1)}, bf16[16,1664]{1,0:T(8,128)(2,1)S(1)}, u32[]{:S(2)}, u32[]{:S(2)}) collective-permute-start(bf16[16,1664]{1,0:T(8,128)(2,1)S(1)} %copy-done.2), channel_id=1, source_target_pairs={{0,2},{2,0},{1,3},{3,1},{4,6},{6,4},{5,7},{7,5},{8,10},{10,8},{9,1... | collective-permute-start | bytes 159752 | tf_op jit(solution)/shard_map/ppermute | solution.py:25
  34.5 1.5 %collective-permute-start.6 = (bf16[32,3328]{1,0:T(8,128)(2,1)S(1)}, bf16[32,3328]{1,0:T(8,128)(2,1)S(1)}, u32[]{:S(2)}, u32[]{:S(2)}) collective-permute-start(bf16[32,3328]{1,0:T(8,128)(2,1)S(1)} %get-tuple-element.17.own_ref), channel_id=1, source_target_pairs={{0,1},{1,0},{2,3},{3,2},{4,5},{5,4},{6,7},{7,6},{8,9},{9,8},{10,11... | collective-permute-start | bytes 638984 | tf_op jit(solution)/shard_map/ppermute | solution.py:25
  46.2 7.7 %collective-permute-start.7 = (bf16[16,4096]{1,0:T(8,128)(2,1)S(1)}, bf16[16,4096]{1,0:T(8,128)(2,1)S(1)}, u32[]{:S(2)}, u32[]{:S(2)}) collective-permute-start(bf16[16,4096]{1,0:T(8,128)(2,1)S(1)} %get-tuple-element.19), channel_id=1, source_target_pairs={{0,4},{4,0},{8,12},{12,8},{1,5},{5,1},{9,13},{13,9},{2,6},{6,2},{1... | collective-permute-start | bytes 393224 | tf_op jit(solution)/shard_map/ppermute | solution.py:25
  48.3 12.9 %collective-permute-start.8 = (bf16[16,4096]{1,0:T(8,128)(2,1)S(1)}, bf16[16,4096]{1,0:T(8,128)(2,1)S(1)}, u32[]{:S(2)}, u32[]{:S(2)}) collective-permute-start(bf16[16,4096]{1,0:T(8,128)(2,1)S(1)} %get-tuple-element.20), channel_id=1, source_target_pairs={{0,8},{4,12},{8,0},{12,4},{1,9},{5,13},{9,1},{13,5},{2,10},{6,14},... | collective-permute-start | bytes 393224 | tf_op jit(solution)/shard_map/ppermute | solution.py:25
  50.5 10.7 %collective-permute-start.9 = (bf16[16,4096]{1,0:T(8,128)(2,1)S(1)}, bf16[16,4096]{1,0:T(8,128)(2,1)S(1)}, u32[]{:S(2)}, u32[]{:S(2)}) collective-permute-start(bf16[16,4096]{1,0:T(8,128)(2,1)S(1)} %get-tuple-element.21), channel_id=1, source_target_pairs={{0,12},{4,8},{8,4},{12,0},{1,13},{5,9},{9,5},{13,1},{2,14},{6,10},... | collective-permute-start | bytes 393224 | tf_op jit(solution)/shard_map/ppermute | solution.py:25

commit v2 on v1

v2 whole, which is shorter than its diff:
```python
import functools
import math

import jax
import jax.numpy as jnp
from jax import lax
from jax.experimental import pallas as pl
from jax.experimental.pallas import tpu as pltpu
from jax.sharding import PartitionSpec as P

VMEM = pl.BlockSpec(memory_space=pltpu.VMEM)
PARAMS = pltpu.CompilerParams(vmem_limit_bytes=8 << 20)
NT = (((1,), (1,)), ((), ()))


def partner(index, step, size):
    return index ^ step if size & (size - 1) == 0 else (index + step) % size


def source(index, step, size):
    return index ^ step if size & (size - 1) == 0 else (index + size - step) % size


def exchange(x, axis, step, size):
    return lax.ppermute(x, axis, [(i, partner(i, step, size)) for i in range(size)])


def tiles(width, tile=256):
    return width // tile, width // tile * tile


def load_turned(weight, next_weight, step=512):
    depth, hidden_cols = weight.shape
    step = math.gcd(depth, step)
    parts = depth // step
    ahead = ahead_rows(depth)

    def kernel(hbm_ref, next_hbm, out_ref, turned_ref, next_ref, sems):
        def copy(part):
            span = pl.ds(pl.multiple_of(part * step, step), step)
            return pltpu.make_async_copy(hbm_ref.at[span], out_ref.at[span], sems.at[part])

        for part in range(parts):
            copy(part).start()
        next_copy = pltpu.make_async_copy(next_hbm.at[pl.ds(0, ahead)], next_ref.at[pl.ds(0, ahead)], sems.at[parts])
        next_copy.start()

        def body(part, carry):
            span = pl.ds(pl.multiple_of(part * step, step), step)
            copy(part).wait()
            turned_ref[:, span] = out_ref[span, :].T
            return carry

        lax.fori_loop(0, parts, body, 0)
        next_copy.wait()

    shape = pltpu.VMEM((depth, hidden_cols), jnp.bfloat16)
    return pl.pallas_call(
        kernel,
        out_shape=[shape, pltpu.VMEM((hidden_cols, depth), jnp.bfloat16), shape],
        in_specs=[pl.BlockSpec(memory_space=pltpu.HBM)] * 2,
        out_specs=[VMEM] * 3,
        scratch_shapes=[pltpu.SemaphoreType.DMA((parts + 1,))],
        compiler_params=PARAMS,
        cost_estimate=pl.CostEstimate(flops=0, bytes_accessed=2 * weight.size, transcendentals=0),
        name="load_turned",
    )(weight, next_weight)


def ahead_rows(depth):
    return math.gcd(depth, 2048)


def turn(weight, step=512):
    depth, hidden_cols = weight.shape
    step = math.gcd(depth, step)

    def kernel(weight_ref, out_ref):
        def body(part, carry):
            span = pl.ds(pl.multiple_of(part * step, step), step)
            out_ref[:, span] = weight_ref[span, :].T
            return carry

        lax.fori_loop(0, depth // step, body, 0)

    return pl.pallas_call(
        kernel,
        out_shape=pltpu.VMEM((hidden_cols, depth), jnp.bfloat16),
        in_specs=[VMEM],
        out_specs=VMEM,
        compiler_params=PARAMS,
        cost_estimate=pl.CostEstimate(flops=0, bytes_accessed=2 * 2 * weight.size, transcendentals=0),
        name="turn",
    )(weight)


def forward(blocks, gate_weight, up_weight, up_buffer, held, sizes):
    wide, narrow, sub = sizes
    block_rows, depth = blocks[0].shape
    hidden_cols = gate_weight.shape[1]
    rows = block_rows * wide
    share = rows // (narrow * sub)
    piece = math.gcd(block_rows, share)
    half = rows // sub
    chunk = ahead_rows(depth)

    def kernel(*refs):
        block_refs = refs[:wide]
        gate_ref, up_hbm, _, _, keep_ref, send_ref, up_ref, x_ref, sems = refs[wide:]
        copies = []
        for i in range(1, depth // chunk):
            span = pl.ds(i * chunk, chunk)
            copies.append(pltpu.make_async_copy(up_hbm.at[span], up_ref.at[span], sems.at[i]))
            copies[-1].start()
        me, core = lax.axis_index("wide"), lax.axis_index("sub")
        for step, block in enumerate(block_refs):
            owner = source(me, step, wide)
            for i in range(block_rows // piece):
                row = owner * block_rows + i * piece
                part = row // share
                place = ((part % sub) ^ core) * half + part // sub * share + row % share
                x_ref[pl.ds(pl.multiple_of(place, piece), piece), :] = block[pl.ds(i * piece, piece), :]

        def columns(weight, start, out, first, last):
            for begin in range(0, hidden_cols, 256):
                width = min(256, hidden_cols - begin)
                product = jnp.dot(
                    x_ref[:, first:last], weight[first:last, begin : begin + width], preferred_element_type=jnp.float32
                )
                cols = pl.ds(out + begin, width)
                if first == start:
                    keep_ref[:, cols] = product[:half]
                    send_ref[:, cols] = product[half:]
                else:
                    keep_ref[:, cols] += product[:half]
                    send_ref[:, cols] += product[half:]

        columns(gate_ref, 0, 0, 0, depth)
        for i in range(depth // chunk):
            if i > 0:
                copies[i - 1].wait()
            columns(up_ref, 0, hidden_cols, i * chunk, (i + 1) * chunk)

    shape = jax.ShapeDtypeStruct((half, 2 * hidden_cols), jnp.float32)
    return pl.pallas_call(
        kernel,
        out_shape=[shape] * 2 + [pltpu.VMEM((depth, hidden_cols), jnp.bfloat16)],
        in_specs=[VMEM] * (wide + 1) + [pl.BlockSpec(memory_space=pltpu.HBM), VMEM, VMEM],
        input_output_aliases={wide + 2: 2},
        out_specs=[VMEM] * 3,
        scratch_shapes=[pltpu.VMEM((rows, depth), jnp.bfloat16), pltpu.SemaphoreType.DMA((depth // chunk,))],
        compiler_params=PARAMS,
        name="forward",
    )(*blocks, gate_weight, up_weight, up_buffer, held)


def activate(own, others, grads, sizes):
    wide, narrow, sub = sizes
    rows, both = own.shape
    hidden_cols = both // 2
    share = rows // narrow

    def kernel(*refs):
        own_ref = refs[0]
        other_refs = refs[1:narrow]
        grad_refs = refs[narrow : 2 * narrow]
        hidden_ref, pre_ref = refs[2 * narrow :]
        me = lax.axis_index("narrow")
        for step, grad_ref in enumerate(grad_refs):
            row = pl.ds(pl.multiple_of(source(me, step, narrow) * share, share), share)

            def total(cols, row=row):
                value = own_ref[row, cols]
                for other in other_refs:
                    value += other[row, cols].astype(jnp.float32)
                return value

            for start in range(0, hidden_cols, 128):
                cols = pl.ds(start, 128)
                up_cols = pl.ds(start + hidden_cols, 128)
                gate, up = total(cols), total(up_cols)
                sig = 1.0 / (1.0 + jnp.exp(-gate))
                act = gate * sig
                if step == 0:
                    hidden_ref[:, cols] = (act * up).astype(jnp.bfloat16)
                grad = grad_ref[:, cols].astype(jnp.float32)
                pre_ref[row, cols] = (grad * up * sig * (1.0 + gate * (1.0 - sig))).astype(jnp.bfloat16)
                pre_ref[row, up_cols] = (grad * act).astype(jnp.bfloat16)

    return pl.pallas_call(
        kernel,
        out_shape=[
            jax.ShapeDtypeStruct((share, hidden_cols), jnp.bfloat16),
            jax.ShapeDtypeStruct((rows, both), jnp.bfloat16),
        ],
        in_specs=[VMEM] * (2 * narrow),
        out_specs=[VMEM] * 2,
        compiler_params=PARAMS,
        name="activate",
    )(own, *others, *grads)


def backward(own, other, gate_turned, up_turned, begin, depth, groups, sizes):
    wide, narrow, sub = sizes
    half, both = own.shape
    hidden_cols = both // 2
    rows = half * sub
    block_rows = rows // wide
    share = half // narrow
    piece = math.gcd(block_rows, share)
    tile = math.gcd(depth, 512)

    def kernel(own_ref, other_ref, gate_ref, up_ref, *refs):
        out_refs, pre_ref = refs[:-1], refs[-1]
        me, core = lax.axis_index("wide"), lax.axis_index("sub")
        for flip, ref in enumerate((own_ref, other_ref)):
            for i in range(half // piece):
                row = (i * piece // share * sub + (core ^ flip)) * share + i * piece % share
                place = source(row // block_rows, me, wide) * block_rows + row % block_rows
                pre_ref[pl.ds(pl.multiple_of(place, piece), piece), :] = ref[pl.ds(i * piece, piece), :]

        for start in range(0, depth, tile):
            from_cols, cols = pl.ds(begin + start, tile), pl.ds(start, tile)
            product = jnp.dot(pre_ref[:, :hidden_cols], gate_ref[:, from_cols], preferred_element_type=jnp.float32)
            product += jnp.dot(pre_ref[:, hidden_cols:], up_ref[:, from_cols], preferred_element_type=jnp.float32)
            for (steps, dtype), out in zip(groups, out_refs):
                for i, step in enumerate(steps):
                    block = product[step * block_rows : (step + 1) * block_rows].astype(dtype)
                    out[i * block_rows : (i + 1) * block_rows, cols] = block

    return pl.pallas_call(
        kernel,
        out_shape=[jax.ShapeDtypeStruct((len(steps) * block_rows, depth), dtype) for steps, dtype in groups],
        in_specs=[VMEM] * 4,
        out_specs=[VMEM] * len(groups),
        scratch_shapes=[pltpu.VMEM((rows, both), jnp.bfloat16)],
        compiler_params=PARAMS,
        cost_estimate=pl.CostEstimate(
            flops=2 * rows * both * depth, bytes_accessed=2 * both * depth, transcendentals=0
        ),
        name="backward",
    )(own, other, gate_turned, up_turned)


def shards(tokens, gate_weight, up_weight, hidden_grad, sizes):
    wide, narrow, sub = sizes
    order = list(AG_ORDER) if wide == 4 else list(range(1, wide))
    got = {step: exchange(tokens, "wide", step, wide) for step in order}
    blocks = [tokens] + [got[step] for step in range(1, wide)]
    gate_weight = pltpu.with_memory_space_constraint(gate_weight, pltpu.HBM)
    up_weight = pltpu.with_memory_space_constraint(up_weight, pltpu.HBM)
    grads = [hidden_grad] + [exchange(hidden_grad, "narrow", step, narrow) for step in range(1, narrow)]
    gate_weight, gate_turned, up_buffer = load_turned(gate_weight, up_weight)
    blocks, grads = lax.optimization_barrier((blocks, grads))
    keep, send, up_weight = forward(blocks, gate_weight, up_weight, up_buffer, gate_turned, sizes)
    chip = keep + exchange(send, "sub", 1, sub)
    chip_bf16 = chip.astype(jnp.bfloat16)
    up_weight, chip_bf16 = lax.optimization_barrier((up_weight, chip_bf16))
    others = [exchange(chip_bf16, "narrow", step, narrow) for step in range(1, narrow)]
    up_turned = turn(up_weight)
    others, up_turned = lax.optimization_barrier((others, up_turned))
    hidden, pre = activate(chip, others, grads, sizes)
    pre_other = exchange(pre, "sub", 1, sub)

    order = list(RS_ORDER) if wide == 4 else list(range(1, wide))
    f32, bf16 = jnp.float32, jnp.bfloat16
    bwd = functools.partial(backward, pre, pre_other, gate_turned, up_turned, sizes=sizes)
    direct = [((0,), f32)] + [((step,), bf16) for step in order]
    depth = tokens.shape[1]
    widths = [depth * share // sum(SHARES) for share in SHARES]
    begins = [sum(widths[:i]) for i in range(len(widths))]
    totals, owns, sends = [], [], []
    for begin, width in zip(begins, widths):
        own, *send = bwd(begin=begin, depth=width, groups=direct)
        owns.append(own)
        sends.append(dict(zip(order, send)))
    whole = {}
    if MERGE:
        whole[1] = exchange(jnp.concatenate([send.pop(1) for send in sends], axis=1), "wide", 1, wide)
    got = [{step: exchange(x, "wide", step, wide) for step, x in send.items()} for send in sends]
    for begin, width, own, parts in zip(begins, widths, owns, got):
        parts.update({step: x[:, begin : begin + width] for step, x in whole.items()})
        totals.append(own + sum(x.astype(f32) for x in parts.values()))
    return (hidden, jnp.concatenate([total.astype(bf16) for total in totals], axis=1))


SHARES = (1, 1)
AG_ORDER = (2, 3, 1)
RS_ORDER = (3, 1, 2)
RELAY = False
MERGE = False


def solution(mesh):
    sizes = tuple(mesh.shape[axis] for axis in ("wide", "narrow", "sub"))
    return jax.shard_map(
        functools.partial(shards, sizes=sizes),
        mesh=mesh,
        in_specs=(
            P(("groups", "wide"), ("narrow", "sub")),
            P(("narrow", "sub"), "wide"),
            P(("narrow", "sub"), "wide"),
            P(("groups", "narrow", "sub"), "wide"),
        ),
        out_specs=(
            P(("groups", "narrow", "sub"), "wide"),
            P(("groups", "wide"), ("narrow", "sub")),
        ),
        check_vma=False,
    )
```

time: 62 us -> 51.2 us (0.83)
  waiting for transfers between devices: 20.3 us -> 9.23 us
  starting transfers between devices: 12.3 us -> 18.3 us
  local copies, waits for them, and re-layouts: 4.88 us -> 0.01 us
  Pallas kernels: 22.9 us -> 21.9 us
    ppermute x10 -> x13, waiting for transfers between devices: 20.3 us -> 9.23 us  [exchange(): lax.ppermute(x, axis, [(i, partner(i, step, size)) for i in range(size)])]
    ppermute x10 -> x13, starting transfers between devices: 12.3 us -> 18.3 us  [exchange(): lax.ppermute(x, axis, [(i, partner(i, step, size)) for i in range(size)])]
    unnamed x6 -> x4, local copies, waits for them, and re-layouts: 4.88 us -> 0.01 us
    pallas_call x3 -> x5, Pallas kernels: 22.2 us -> 21.2 us  [the longest x1 6.98 us: load_turned(): pl.pallas_call(kernel, out_shape=[shape, pltpu.VMEM((hidden_cols, depth),...]
    concatenate x0 -> x1, other arithmetic: none -> 0.67 us  [shards(): jnp.concatenate([total.astype(bf16) for total in totals], axis=1)]
    convert_element_type x1 -> x2, other arithmetic: 0.72 us -> 0.07 us  [shards(): total.astype(bf16)]
  transfers between devices with their start and end apart: 10 -> 13, of which waited for: 6 -> 7; matrix products, arithmetic and copies ran while one was open for 0% -> 0% of each run, Pallas kernels for 9% -> 27%
where the time goes in v2:
time: 51.2 us; the launch traced here: 51 us
  Pallas kernels  21.9 us (43%)
  starting transfers between devices  18.3 us (36%)
  waiting for transfers between devices  9.23 us (18%)
  other arithmetic  0.8 us (2%)
  between operations  0.74 us (1%)
    ppermute x13, starting transfers between devices, exchange(): lax.ppermute(x, axis, [(i, partner(i, step, size)) for i in range(size)])  18.3 us
    ppermute x13, waiting for transfers between devices, exchange(): lax.ppermute(x, axis, [(i, partner(i, step, size)) for i in range(size)])  9.23 us
    pallas_call x1, Pallas kernels, load_turned(): pl.pallas_call(kernel, out_shape=[shape, pltpu.VMEM((hidden_cols, depth),...  6.98 us
    pallas_call x2, Pallas kernels, backward(): pl.pallas_call(kernel, out_shape=[jax.ShapeDtypeStruct((len(steps) * bloc...  5.01 us
    pallas_call x1, Pallas kernels, forward(): pl.pallas_call(kernel, out_shape=[shape] * 2 + [pltpu.VMEM((depth, hidden...  4.96 us
    pallas_call x1, Pallas kernels, turn(): pl.pallas_call(kernel, out_shape=pltpu.VMEM((hidden_cols, depth), jnp.bfl...  4.24 us
  transfers between devices with their start and end apart: 13, of which 7 were waited for; matrix products, arithmetic and copies ran while one was open for 0% of the time, Pallas kernels for 27%

profile of v2, /device:TPU:0, one launch (start us, length us, event | category | flops | bytes accessed | tf_op | source)
XLA Modules:
  0.0 51.0 jit_solution(2907928243946234051)
XLA Ops:
  0.6 0.0 copy-start
  0.6 4.1 %collective-permute-start.1 = (bf16[16,4096]{1,0:T(8,128)(2,1)}, bf16[16,4096]{1,0:T(8,128)(2,1)S(1)}, u32[]{:S(2)}, u32[]{:S(2)}) collective-permute-start(bf16[16,4096]{1,0:T(8,128)(2,1)} %refs_0_), channel_id=1, source_target_pairs={{0,8},{4,12},{8,0},{12,4},{1,9},{5,13},{9,1},{13,5},{2,10},{6,14},... | collective-permute-start | bytes 393224 | tf_op jit(solution)/shard_map/ppermute | solution.py:25
  4.7 1.6 %collective-permute-start = (bf16[16,4096]{1,0:T(8,128)(2,1)}, bf16[16,4096]{1,0:T(8,128)(2,1)S(1)}, u32[]{:S(2)}, u32[]{:S(2)}) collective-permute-start(bf16[16,4096]{1,0:T(8,128)(2,1)} %refs_0_), channel_id=1, source_target_pairs={{0,4},{4,0},{8,12},{12,8},{1,5},{5,1},{9,13},{13,9},{2,6},{6,2},{1... | collective-permute-start | bytes 393224 | tf_op jit(solution)/shard_map/ppermute | solution.py:25
  6.3 0.0 collective-permute-start.2
  6.3 1.7 %collective-permute-start.3 = (bf16[16,1664]{1,0:T(8,128)(2,1)}, bf16[16,1664]{1,0:T(8,128)(2,1)S(1)}, u32[]{:S(2)}, u32[]{:S(2)}) collective-permute-start(bf16[16,1664]{1,0:T(8,128)(2,1)} %refs_2_), channel_id=1, source_target_pairs={{0,2},{2,0},{1,3},{3,1},{4,6},{6,4},{5,7},{7,5},{8,10},{10,8},{9,1... | collective-permute-start | bytes 159752 | tf_op jit(solution)/shard_map/ppermute | solution.py:25
  8.0 7.0 %load_turned.1 = (bf16[4096,1664]{1,0:T(8,128)(2,1)S(1)}, bf16[1664,4096]{1,0:T(8,128)(2,1)S(1)}, bf16[4096,1664]{1,0:T(8,128)(2,1)S(1)}) custom-call(bf16[4096,1664]{1,0:T(8,128)(2,1)} %hbm_ref.1, bf16[4096,1664]{1,0:T(8,128)(2,1)} %refs_5_.1), custom_call_target="tpu_custom_call" | custom-call | bytes 13631488 | tf_op jit(solution)/shard_map/load_turned/pallas_call | solution.py:58
  15.0 0.0 collective-permute-done.3.refs_3_
  15.0 0.0 collective-permute-done.1.refs_2_
  15.0 0.0 collective-permute-done.refs_1_
  15.1 0.2 collective-permute-done.2.refs_3_
  15.3 0.0 copy-done
  15.3 5.0 %forward.1 = (f32[32,3328]{1,0:T(8,128)S(1)}, f32[32,3328]{1,0:T(8,128)S(1)}, bf16[4096,1664]{1,0:T(8,128)(2,1)S(1)}) custom-call(bf16[16,4096]{1,0:T(8,128)(2,1)S(1)} %copy-done, bf16[16,4096]{1,0:T(8,128)(2,1)S(1)} %collective-permute-done.refs_1_, bf16[16,4096]{1,0:T(8,128)(2,1)S(1)} %collective-permute-done.1.refs_2_, ...), custom_call_target="tpu_custom_call", output_to_operand_aliasing={{2}: (6, {})} | custom-call | tf_op jit(solution)/shard_map/forward/pallas_call | solution.py:145
  20.3 0.1 collective-permute-start.4
  20.3 1.8 %collective-permute-done.4 = f32[32,3328]{1,0:T(8,128)S(1)} collective-permute-done((f32[32,3328]{1,0:T(8,128)S(1)}, f32[32,3328]{1,0:T(8,128)S(1)}, u32[]{:S(2)}, u32[]{:S(2)}) %collective-permute-start.4) | collective-permute-done | bytes 426016 | tf_op jit(solution)/shard_map/ppermute | solution.py:25
  22.1 0.1 fusion
  22.2 0.0 copy-start.1
  22.2 1.6 %collective-permute-start.5 = (bf16[32,3328]{1,0:T(8,128)(2,1)S(1)}, bf16[32,3328]{1,0:T(8,128)(2,1)S(1)}, u32[]{:S(2)}, u32[]{:S(2)}) collective-permute-start(bf16[32,3328]{1,0:T(8,128)(2,1)S(1)} %get-tuple-element.38), channel_id=1, source_target_pairs={{0,2},{2,0},{1,3},{3,1},{4,6},{6,4},{5,7},{7,5},{8,10},{10,8},{9,1... | collective-permute-start | bytes 638984 | tf_op jit(solution)/shard_map/ppermute | solution.py:25
  23.7 4.2 %turn.1.up_ref = bf16[1664,4096]{1,0:T(8,128)(2,1)S(1)} custom-call(bf16[4096,1664]{1,0:T(8,128)(2,1)S(1)} %get-tuple-element.39.weight_ref), custom_call_target="tpu_custom_call" | custom-call | bytes 27262976 | tf_op jit(solution)/shard_map/turn/pallas_call | solution.py:86
  28.0 1.5 %collective-permute-done.5.refs_1_ = bf16[32,3328]{1,0:T(8,128)(2,1)S(1)} collective-permute-done((bf16[32,3328]{1,0:T(8,128)(2,1)S(1)}, bf16[32,3328]{1,0:T(8,128)(2,1)S(1)}, u32[]{:S(2)}, u32[]{:S(2)}) %collective-permute-start.5) | collective-permute-done | bytes 213024 | tf_op jit(solution)/shard_map/ppermute | solution.py:25
  29.5 0.0 copy-done.1
  29.5 0.7 %activate.1 = (bf16[16,1664]{1,0:T(8,128)(2,1)}, bf16[32,3328]{1,0:T(8,128)(2,1)S(1)}) custom-call(f32[32,3328]{1,0:T(8,128)S(1)} %get-tuple-element.55.refs_0_, bf16[32,3328]{1,0:T(8,128)(2,1)S(1)} %collective-permute-done.5.refs_1_, bf16[16,1664]{1,0:T(8,128)(2,1)S(1)} %copy-done.1, bf16[16,1664]{1,0:T(8,128)(2,1)S(1)} %collective-permute-done.3.refs_3_), custom_call_target="tpu_custom_call" | custom-call | tf_op jit(solution)/shard_map/activate/pallas_call | solution.py:190
  30.2 0.0 collective-permute-start.6
  30.2 1.5 %collective-permute-done.6.other_ref = bf16[32,3328]{1,0:T(8,128)(2,1)S(1)} collective-permute-done((bf16[32,3328]{1,0:T(8,128)(2,1)S(1)}, bf16[32,3328]{1,0:T(8,128)(2,1)S(1)}, u32[]{:S(2)}, u32[]{:S(2)}) %collective-permute-start.6) | collective-permute-done | bytes 213024 | tf_op jit(solution)/shard_map/ppermute | solution.py:25
  31.7 2.5 %backward.3 = (f32[16,2048]{1,0:T(8,128)S(1)}, bf16[16,2048]{1,0:T(8,128)(2,1)S(1)}, bf16[16,2048]{1,0:T(8,128)(2,1)S(1)}, bf16[16,2048]{1,0:T(8,128)(2,1)S(1)}) custom-call(bf16[32,3328]{1,0:T(8,128)(2,1)S(1)} %get-tuple-element.44.own_ref, bf16[32,3328]{1,0:T(8,128)(2,1)S(1)} %collective-permute-done.6.other_ref, ...), custom_call_target="tpu_custom_call" | custom-call | flops 872415232 | bytes 13631488 | tf_op jit(solution)/shard_map/backward/pallas_call | solution.py:231
  34.2 3.5 %collective-permute-start.10 = (bf16[16,2048]{1,0:T(8,128)(2,1)S(1)}, bf16[16,2048]{1,0:T(8,128)(2,1)S(1)}, u32[]{:S(2)}, u32[]{:S(2)}) collective-permute-start(bf16[16,2048]{1,0:T(8,128)(2,1)S(1)} %get-tuple-element.51), channel_id=1, source_target_pairs={{0,12},{4,8},{8,4},{12,0},{1,13},{5,9},{9,5},{13,1},{2,14},{6,10},... | collective-permute-start | bytes 196616 | tf_op jit(solution)/shard_map/ppermute | solution.py:25
  37.7 1.4 %collective-permute-start.11 = (bf16[16,2048]{1,0:T(8,128)(2,1)S(1)}, bf16[16,2048]{1,0:T(8,128)(2,1)S(1)}, u32[]{:S(2)}, u32[]{:S(2)}) collective-permute-start(bf16[16,2048]{1,0:T(8,128)(2,1)S(1)} %get-tuple-element.52), channel_id=1, source_target_pairs={{0,4},{4,0},{8,12},{12,8},{1,5},{5,1},{9,13},{13,9},{2,6},{6,2},{1... | collective-permute-start | bytes 196616 | tf_op jit(solution)/shard_map/ppermute | solution.py:25
  39.1 0.0 collective-permute-start.12
  39.1 2.5 %backward.2 = (f32[16,2048]{1,0:T(8,128)S(1)}, bf16[16,2048]{1,0:T(8,128)(2,1)S(1)}, bf16[16,2048]{1,0:T(8,128)(2,1)S(1)}, bf16[16,2048]{1,0:T(8,128)(2,1)S(1)}) custom-call(bf16[32,3328]{1,0:T(8,128)(2,1)S(1)} %get-tuple-element.44.own_ref, bf16[32,3328]{1,0:T(8,128)(2,1)S(1)} %collective-permute-done.6.other_ref, ...), custom_call_target="tpu_custom_call" | custom-call | flops 872415232 | bytes 13631488 | tf_op jit(solution)/shard_map/backward/pallas_call | solution.py:231
  41.6 3.1 %collective-permute-start.7 = (bf16[16,2048]{1,0:T(8,128)(2,1)S(1)}, bf16[16,2048]{1,0:T(8,128)(2,1)S(1)}, u32[]{:S(2)}, u32[]{:S(2)}) collective-permute-start(bf16[16,2048]{1,0:T(8,128)(2,1)S(1)} %get-tuple-element.47), channel_id=1, source_target_pairs={{0,12},{4,8},{8,4},{12,0},{1,13},{5,9},{9,5},{13,1},{2,14},{6,10},... | collective-permute-start | bytes 196616 | tf_op jit(solution)/shard_map/ppermute | solution.py:25
  44.7 0.5 collective-permute-start.8
  45.1 0.0 collective-permute-done.10
  45.2 0.9 %collective-permute-start.9 = (bf16[16,2048]{1,0:T(8,128)(2,1)S(1)}, bf16[16,2048]{1,0:T(8,128)(2,1)S(1)}, u32[]{:S(2)}, u32[]{:S(2)}) collective-permute-start(bf16[16,2048]{1,0:T(8,128)(2,1)S(1)} %get-tuple-element.49), channel_id=1, source_target_pairs={{0,8},{4,12},{8,0},{12,4},{1,9},{5,13},{9,1},{13,5},{2,10},{6,14},... | collective-permute-start | bytes 196616 | tf_op jit(solution)/shard_map/ppermute | solution.py:25
  46.1 0.0 collective-permute-done.11
  46.1 0.0 collective-permute-done.12
  46.1 1.7 %collective-permute-done.7 = bf16[16,2048]{1,0:T(8,128)(2,1)S(1)} collective-permute-done((bf16[16,2048]{1,0:T(8,128)(2,1)S(1)}, bf16[16,2048]{1,0:T(8,128)(2,1)S(1)}, u32[]{:S(2)}, u32[]{:S(2)}) %collective-permute-start.7) | collective-permute-done | bytes 65568 | tf_op jit(solution)/shard_map/ppermute | solution.py:25
  47.8 1.4 %collective-permute-done.8 = bf16[16,2048]{1,0:T(8,128)(2,1)S(1)} collective-permute-done((bf16[16,2048]{1,0:T(8,128)(2,1)S(1)}, bf16[16,2048]{1,0:T(8,128)(2,1)S(1)}, u32[]{:S(2)}, u32[]{:S(2)}) %collective-permute-start.8) | collective-permute-done | bytes 65568 | tf_op jit(solution)/shard_map/ppermute | solution.py:25
  49.2 1.1 %collective-permute-done.9 = bf16[16,2048]{1,0:T(8,128)(2,1)S(1)} collective-permute-done((bf16[16,2048]{1,0:T(8,128)(2,1)S(1)}, bf16[16,2048]{1,0:T(8,128)(2,1)S(1)}, u32[]{:S(2)}, u32[]{:S(2)}) %collective-permute-start.9) | collective-permute-done | bytes 65568 | tf_op jit(solution)/shard_map/ppermute | solution.py:25
  50.4 0.7 %pad_maximum_fusion = bf16[16,4096]{1,0:T(8,128)(2,1)} fusion(bf16[16,2048]{1,0:T(8,128)(2,1)S(1)} %add_convert_fusion, bf16[16,2048]{1,0:T(8,128)(2,1)S(1)} %add_convert_fusion.1), kind=kLoop, calls=%fused_computation | loop fusion | flops 262144 | bytes 262144 | tf_op jit(solution)/shard_map/concatenate | solution.py:284
  (2 shorter events, 0.1 us)
Async XLA Ops:
  0.6 14.7 %copy-start = (bf16[16,4096]{1,0:T(8,128)(2,1)S(1)}, bf16[16,4096]{1,0:T(8,128)(2,1)}, u32[]{:S(2)}) copy-start(bf16[16,4096]{1,0:T(8,128)(2,1)} %refs_0_) | copy-start | bytes 393220
  0.6 14.4 %collective-permute-start.1 = (bf16[16,4096]{1,0:T(8,128)(2,1)}, bf16[16,4096]{1,0:T(8,128)(2,1)S(1)}, u32[]{:S(2)}, u32[]{:S(2)}) collective-permute-start(bf16[16,4096]{1,0:T(8,128)(2,1)} %refs_0_), channel_id=1, source_target_pairs={{0,8},{4,12},{8,0},{12,4},{1,9},{5,13},{9,1},{13,5},{2,10},{6,14},... | collective-permute-start | bytes 393224 | tf_op jit(solution)/shard_map/ppermute | solution.py:25
  4.7 10.3 %collective-permute-start = (bf16[16,4096]{1,0:T(8,128)(2,1)}, bf16[16,4096]{1,0:T(8,128)(2,1)S(1)}, u32[]{:S(2)}, u32[]{:S(2)}) collective-permute-start(bf16[16,4096]{1,0:T(8,128)(2,1)} %refs_0_), channel_id=1, source_target_pairs={{0,4},{4,0},{8,12},{12,8},{1,5},{5,1},{9,13},{13,9},{2,6},{6,2},{1... | collective-permute-start | bytes 393224 | tf_op jit(solution)/shard_map/ppermute | solution.py:25
  6.3 9.0 %collective-permute-start.2 = (bf16[16,4096]{1,0:T(8,128)(2,1)}, bf16[16,4096]{1,0:T(8,128)(2,1)S(1)}, u32[]{:S(2)}, u32[]{:S(2)}) collective-permute-start(bf16[16,4096]{1,0:T(8,128)(2,1)} %refs_0_), channel_id=1, source_target_pairs={{0,12},{4,8},{8,4},{12,0},{1,13},{5,9},{9,5},{13,1},{2,14},{6,10},... | collective-permute-start | bytes 393224 | tf_op jit(solution)/shard_map/ppermute | solution.py:25
  6.3 8.7 %collective-permute-start.3 = (bf16[16,1664]{1,0:T(8,128)(2,1)}, bf16[16,1664]{1,0:T(8,128)(2,1)S(1)}, u32[]{:S(2)}, u32[]{:S(2)}) collective-permute-start(bf16[16,1664]{1,0:T(8,128)(2,1)} %refs_2_), channel_id=1, source_target_pairs={{0,2},{2,0},{1,3},{3,1},{4,6},{6,4},{5,7},{7,5},{8,10},{10,8},{9,1... | collective-permute-start | bytes 159752 | tf_op jit(solution)/shard_map/ppermute | solution.py:25
  20.3 1.8 %collective-permute-start.4 = (f32[32,3328]{1,0:T(8,128)S(1)}, f32[32,3328]{1,0:T(8,128)S(1)}, u32[]{:S(2)}, u32[]{:S(2)}) collective-permute-start(f32[32,3328]{1,0:T(8,128)S(1)} %get-tuple-element.36), channel_id=1, source_target_pairs={{0,1},{1,0},{2,3},{3,2},{4,5},{5,4},{6,7},{7,6},{8,9},{9,8},{10,11... | collective-permute-start | bytes 1277960 | tf_op jit(solution)/shard_map/ppermute | solution.py:25
  22.2 7.4 %copy-start.1 = (bf16[16,1664]{1,0:T(8,128)(2,1)S(1)}, bf16[16,1664]{1,0:T(8,128)(2,1)}, u32[]{:S(2)}) copy-start(bf16[16,1664]{1,0:T(8,128)(2,1)} %refs_2_) | copy-start | bytes 159748
  22.2 7.4 %collective-permute-start.5 = (bf16[32,3328]{1,0:T(8,128)(2,1)S(1)}, bf16[32,3328]{1,0:T(8,128)(2,1)S(1)}, u32[]{:S(2)}, u32[]{:S(2)}) collective-permute-start(bf16[32,3328]{1,0:T(8,128)(2,1)S(1)} %get-tuple-element.38), channel_id=1, source_target_pairs={{0,2},{2,0},{1,3},{3,1},{4,6},{6,4},{5,7},{7,5},{8,10},{10,8},{9,1... | collective-permute-start | bytes 638984 | tf_op jit(solution)/shard_map/ppermute | solution.py:25
  30.2 1.5 %collective-permute-start.6 = (bf16[32,3328]{1,0:T(8,128)(2,1)S(1)}, bf16[32,3328]{1,0:T(8,128)(2,1)S(1)}, u32[]{:S(2)}, u32[]{:S(2)}) collective-permute-start(bf16[32,3328]{1,0:T(8,128)(2,1)S(1)} %get-tuple-element.44.own_ref), channel_id=1, source_target_pairs={{0,1},{1,0},{2,3},{3,2},{4,5},{5,4},{6,7},{7,6},{8,9},{9,8},{10,11... | collective-permute-start | bytes 638984 | tf_op jit(solution)/shard_map/ppermute | solution.py:25
  34.2 10.9 %collective-permute-start.10 = (bf16[16,2048]{1,0:T(8,128)(2,1)S(1)}, bf16[16,2048]{1,0:T(8,128)(2,1)S(1)}, u32[]{:S(2)}, u32[]{:S(2)}) collective-permute-start(bf16[16,2048]{1,0:T(8,128)(2,1)S(1)} %get-tuple-element.51), channel_id=1, source_target_pairs={{0,12},{4,8},{8,4},{12,0},{1,13},{5,9},{9,5},{13,1},{2,14},{6,10},... | collective-permute-start | bytes 196616 | tf_op jit(solution)/shard_map/ppermute | solution.py:25
  37.7 8.4 %collective-permute-start.11 = (bf16[16,2048]{1,0:T(8,128)(2,1)S(1)}, bf16[16,2048]{1,0:T(8,128)(2,1)S(1)}, u32[]{:S(2)}, u32[]{:S(2)}) collective-permute-start(bf16[16,2048]{1,0:T(8,128)(2,1)S(1)} %get-tuple-element.52), channel_id=1, source_target_pairs={{0,4},{4,0},{8,12},{12,8},{1,5},{5,1},{9,13},{13,9},{2,6},{6,2},{1... | collective-permute-start | bytes 196616 | tf_op jit(solution)/shard_map/ppermute | solution.py:25
  39.1 7.0 %collective-permute-start.12 = (bf16[16,2048]{1,0:T(8,128)(2,1)S(1)}, bf16[16,2048]{1,0:T(8,128)(2,1)S(1)}, u32[]{:S(2)}, u32[]{:S(2)}) collective-permute-start(bf16[16,2048]{1,0:T(8,128)(2,1)S(1)} %get-tuple-element.53), channel_id=1, source_target_pairs={{0,8},{4,12},{8,0},{12,4},{1,9},{5,13},{9,1},{13,5},{2,10},{6,14},... | collective-permute-start | bytes 196616 | tf_op jit(solution)/shard_map/ppermute | solution.py:25
  41.6 6.2 %collective-permute-start.7 = (bf16[16,2048]{1,0:T(8,128)(2,1)S(1)}, bf16[16,2048]{1,0:T(8,128)(2,1)S(1)}, u32[]{:S(2)}, u32[]{:S(2)}) collective-permute-start(bf16[16,2048]{1,0:T(8,128)(2,1)S(1)} %get-tuple-element.47), channel_id=1, source_target_pairs={{0,12},{4,8},{8,4},{12,0},{1,13},{5,9},{9,5},{13,1},{2,14},{6,10},... | collective-permute-start | bytes 196616 | tf_op jit(solution)/shard_map/ppermute | solution.py:25
  44.7 4.5 %collective-permute-start.8 = (bf16[16,2048]{1,0:T(8,128)(2,1)S(1)}, bf16[16,2048]{1,0:T(8,128)(2,1)S(1)}, u32[]{:S(2)}, u32[]{:S(2)}) collective-permute-start(bf16[16,2048]{1,0:T(8,128)(2,1)S(1)} %get-tuple-element.48), channel_id=1, source_target_pairs={{0,4},{4,0},{8,12},{12,8},{1,5},{5,1},{9,13},{13,9},{2,6},{6,2},{1... | collective-permute-start | bytes 196616 | tf_op jit(solution)/shard_map/ppermute | solution.py:25
  45.2 5.2 %collective-permute-start.9 = (bf16[16,2048]{1,0:T(8,128)(2,1)S(1)}, bf16[16,2048]{1,0:T(8,128)(2,1)S(1)}, u32[]{:S(2)}, u32[]{:S(2)}) collective-permute-start(bf16[16,2048]{1,0:T(8,128)(2,1)S(1)} %get-tuple-element.49), channel_id=1, source_target_pairs={{0,8},{4,12},{8,0},{12,4},{1,9},{5,13},{9,1},{13,5},{2,10},{6,14},... | collective-permute-start | bytes 196616 | tf_op jit(solution)/shard_map/ppermute | solution.py:25

commit v3 on v2

--- a/solution.py
+++ b/solution.py
@@ -68,7 +68,7 @@
 
 
 def ahead_rows(depth):
-    return math.gcd(depth, 2048)
+    return depth * AHEAD // 4
 
 
 def turn(weight, step=512):
@@ -94,7 +94,7 @@
     )(weight)
 
 
-def forward(blocks, gate_weight, up_weight, up_buffer, held, sizes):
+def forward(steps, blocks, gate_weight, up_weight, up_buffer, held, sizes):
     wide, narrow, sub = sizes
     block_rows, depth = blocks[0].shape
     hidden_cols = gate_weight.shape[1]
@@ -102,18 +102,16 @@
     share = rows // (narrow * sub)
     piece = math.gcd(block_rows, share)
     half = rows // sub
-    chunk = ahead_rows(depth)
+    ahead = ahead_rows(depth)
 
     def kernel(*refs):
         block_refs = refs[:wide]
-        gate_ref, up_hbm, _, _, keep_ref, send_ref, up_ref, x_ref, sems = refs[wide:]
-        copies = []
-        for i in range(1, depth // chunk):
-            span = pl.ds(i * chunk, chunk)
-            copies.append(pltpu.make_async_copy(up_hbm.at[span], up_ref.at[span], sems.at[i]))
-            copies[-1].start()
+        gate_ref, up_hbm, _, _, keep_ref, send_ref, up_ref, x_ref, sem = refs[wide:]
+        span = pl.ds(ahead, depth - ahead)
+        rest = pltpu.make_async_copy(up_hbm.at[span], up_ref.at[span], sem)
+        rest.start()
         me, core = lax.axis_index("wide"), lax.axis_index("sub")
-        for step, block in enumerate(block_refs):
+        for step, block in zip(steps, block_refs):
             owner = source(me, step, wide)
             for i in range(block_rows // piece):
                 row = owner * block_rows + i * piece
@@ -121,34 +119,30 @@
                 place = ((part % sub) ^ core) * half + part // sub * share + row % share
                 x_ref[pl.ds(pl.multiple_of(place, piece), piece), :] = block[pl.ds(i * piece, piece), :]
 
-        def columns(weight, start, out, first, last):
+        def columns(weight, out):
             for begin in range(0, hidden_cols, 256):
                 width = min(256, hidden_cols - begin)
-                product = jnp.dot(
-                    x_ref[:, first:last], weight[first:last, begin : begin + width], preferred_element_type=jnp.float32
-                )
+                product = jnp.dot(x_ref[...], weight[:, begin : begin + width], preferred_element_type=jnp.float32)
                 cols = pl.ds(out + begin, width)
-                if first == start:
-                    keep_ref[:, cols] = product[:half]
-                    send_ref[:, cols] = product[half:]
-                else:
-                    keep_ref[:, cols] += product[:half]
-                    send_ref[:, cols] += product[half:]
-
-        columns(gate_ref, 0, 0, 0, depth)
-        for i in range(depth // chunk):
-            if i > 0:
-                copies[i - 1].wait()
-            columns(up_ref, 0, hidden_cols, i * chunk, (i + 1) * chunk)
-
-    shape = jax.ShapeDtypeStruct((half, 2 * hidden_cols), jnp.float32)
-    return pl.pallas_call(
-        kernel,
-        out_shape=[shape] * 2 + [pltpu.VMEM((depth, hidden_cols), jnp.bfloat16)],
+                keep_ref[:, cols] = product[:half]
+                send_ref[:, cols] = product[half:].astype(send_ref.dtype)
+
+        columns(gate_ref, 0)
+        rest.wait()
+        columns(up_ref, hidden_cols)
+
+    shape = (half, 2 * hidden_cols)
+    return pl.pallas_call(
+        kernel,
+        out_shape=[
+            jax.ShapeDtypeStruct(shape, jnp.float32),
+            jax.ShapeDtypeStruct(shape, SUB_DTYPE),
+            pltpu.VMEM((depth, hidden_cols), jnp.bfloat16),
+        ],
         in_specs=[VMEM] * (wide + 1) + [pl.BlockSpec(memory_space=pltpu.HBM), VMEM, VMEM],
         input_output_aliases={wide + 2: 2},
         out_specs=[VMEM] * 3,
-        scratch_shapes=[pltpu.VMEM((rows, depth), jnp.bfloat16), pltpu.SemaphoreType.DMA((depth // chunk,))],
+        scratch_shapes=[pltpu.VMEM((rows, depth), jnp.bfloat16), pltpu.SemaphoreType.DMA(())],
         compiler_params=PARAMS,
         name="forward",
     )(*blocks, gate_weight, up_weight, up_buffer, held)
@@ -190,7 +184,7 @@
     return pl.pallas_call(
         kernel,
         out_shape=[
-            jax.ShapeDtypeStruct((share, hidden_cols), jnp.bfloat16),
+            pltpu.VMEM((share, hidden_cols), jnp.bfloat16),
             jax.ShapeDtypeStruct((rows, both), jnp.bfloat16),
         ],
         in_specs=[VMEM] * (2 * narrow),
@@ -246,14 +240,15 @@
     wide, narrow, sub = sizes
     order = list(AG_ORDER) if wide == 4 else list(range(1, wide))
     got = {step: exchange(tokens, "wide", step, wide) for step in order}
-    blocks = [tokens] + [got[step] for step in range(1, wide)]
+    steps = [0] + order
+    blocks = [tokens] + [got[step] for step in order]
     gate_weight = pltpu.with_memory_space_constraint(gate_weight, pltpu.HBM)
     up_weight = pltpu.with_memory_space_constraint(up_weight, pltpu.HBM)
     grads = [hidden_grad] + [exchange(hidden_grad, "narrow", step, narrow) for step in range(1, narrow)]
     gate_weight, gate_turned, up_buffer = load_turned(gate_weight, up_weight)
     blocks, grads = lax.optimization_barrier((blocks, grads))
-    keep, send, up_weight = forward(blocks, gate_weight, up_weight, up_buffer, gate_turned, sizes)
-    chip = keep + exchange(send, "sub", 1, sub)
+    keep, send, up_weight = forward(steps, blocks, gate_weight, up_weight, up_buffer, gate_turned, sizes)
+    chip = keep + exchange(send, "sub", 1, sub).astype(jnp.float32)
     chip_bf16 = chip.astype(jnp.bfloat16)
     up_weight, chip_bf16 = lax.optimization_barrier((up_weight, chip_bf16))
     others = [exchange(chip_bf16, "narrow", step, narrow) for step in range(1, narrow)]
@@ -284,8 +279,10 @@
     return (hidden, jnp.concatenate([total.astype(bf16) for total in totals], axis=1))
 
 
+SUB_DTYPE = jnp.bfloat16
+AHEAD = 3
 SHARES = (1, 1)
-AG_ORDER = (2, 3, 1)
+AG_ORDER = (3, 2, 1)
 RS_ORDER = (3, 1, 2)
 RELAY = False
 MERGE = False

time: 51.2 us -> 50.4 us (0.984)
  waiting for transfers between devices: 9.23 us -> 8.31 us
  starting transfers between devices: 18.3 us -> 17.4 us
  local copies, waits for them, and re-layouts: 0.01 us -> 0.63 us
    pallas_call x1, Pallas kernels: 6.98 us -> 7.95 us  [load_turned(): pl.pallas_call(kernel, out_shape=[shape, pltpu.VMEM((hidden_cols, depth),...]
    ppermute x13, waiting for transfers between devices: 9.23 us -> 8.31 us  [exchange(): lax.ppermute(x, axis, [(i, partner(i, step, size)) for i in range(size)])]
    ppermute x13, starting transfers between devices: 18.3 us -> 17.4 us  [exchange(): lax.ppermute(x, axis, [(i, partner(i, step, size)) for i in range(size)])]
    unnamed x4 -> x5, local copies, waits for them, and re-layouts: 0.01 us -> 0.63 us
    pallas_call x2, Pallas kernels: 5.68 us -> 5.12 us  [the longest x1 4.95 us: forward(): pl.pallas_call(kernel, out_shape=[jax.ShapeDtypeStruct(shape, jnp.float32...]
  transfers between devices with their start and end apart: 13 -> 13, of which waited for: 7 -> 6; matrix products, arithmetic and copies ran while one was open for 0% -> 1% of each run, Pallas kernels for 27% -> 29%
where the time goes in v3:
time: 50.4 us; the launch traced here: 50.2 us
  Pallas kernels  22.3 us (44%)
  starting transfers between devices  17.4 us (35%)
  waiting for transfers between devices  8.31 us (16%)
  other arithmetic  0.78 us (2%)
  between operations  0.76 us (2%)
  local copies, waits for them, and re-layouts  0.63 us (1%)
    ppermute x13, starting transfers between devices, exchange(): lax.ppermute(x, axis, [(i, partner(i, step, size)) for i in range(size)])  17.4 us
    ppermute x13, waiting for transfers between devices, exchange(): lax.ppermute(x, axis, [(i, partner(i, step, size)) for i in range(size)])  8.31 us
    pallas_call x1, Pallas kernels, load_turned(): pl.pallas_call(kernel, out_shape=[shape, pltpu.VMEM((hidden_cols, depth),...  7.95 us
    pallas_call x2, Pallas kernels, backward(): pl.pallas_call(kernel, out_shape=[jax.ShapeDtypeStruct((len(steps) * bloc...  5.01 us
    pallas_call x1, Pallas kernels, forward(): pl.pallas_call(kernel, out_shape=[jax.ShapeDtypeStruct(shape, jnp.float32...  4.95 us
    pallas_call x1, Pallas kernels, turn(): pl.pallas_call(kernel, out_shape=pltpu.VMEM((hidden_cols, depth), jnp.bfl...  4.24 us
  transfers between devices with their start and end apart: 13, of which 6 were waited for; matrix products, arithmetic and copies ran while one was open for 1% of the time, Pallas kernels for 29%

profile of v3, /device:TPU:0, one launch (start us, length us, event | category | flops | bytes accessed | tf_op | source)
XLA Modules:
  0.0 50.2 jit_solution(3553216146764095363)
XLA Ops:
  0.6 0.0 copy-start
  0.6 4.1 %collective-permute-start.1 = (bf16[16,4096]{1,0:T(8,128)(2,1)}, bf16[16,4096]{1,0:T(8,128)(2,1)S(1)}, u32[]{:S(2)}, u32[]{:S(2)}) collective-permute-start(bf16[16,4096]{1,0:T(8,128)(2,1)} %refs_0_), channel_id=1, source_target_pairs={{0,8},{4,12},{8,0},{12,4},{1,9},{5,13},{9,1},{13,5},{2,10},{6,14},... | collective-permute-start | bytes 393224 | tf_op jit(solution)/shard_map/ppermute | solution.py:25
  4.7 1.3 %collective-permute-start = (bf16[16,4096]{1,0:T(8,128)(2,1)}, bf16[16,4096]{1,0:T(8,128)(2,1)S(1)}, u32[]{:S(2)}, u32[]{:S(2)}) collective-permute-start(bf16[16,4096]{1,0:T(8,128)(2,1)} %refs_0_), channel_id=1, source_target_pairs={{0,12},{4,8},{8,4},{12,0},{1,13},{5,9},{9,5},{13,1},{2,14},{6,10},... | collective-permute-start | bytes 393224 | tf_op jit(solution)/shard_map/ppermute | solution.py:25
  6.1 0.2 collective-permute-start.2
  6.3 1.5 %collective-permute-start.3 = (bf16[16,1664]{1,0:T(8,128)(2,1)}, bf16[16,1664]{1,0:T(8,128)(2,1)S(1)}, u32[]{:S(2)}, u32[]{:S(2)}) collective-permute-start(bf16[16,1664]{1,0:T(8,128)(2,1)} %refs_2_), channel_id=1, source_target_pairs={{0,2},{2,0},{1,3},{3,1},{4,6},{6,4},{5,7},{7,5},{8,10},{10,8},{9,1... | collective-permute-start | bytes 159752 | tf_op jit(solution)/shard_map/ppermute | solution.py:25
  7.8 8.0 %load_turned.1 = (bf16[4096,1664]{1,0:T(8,128)(2,1)S(1)}, bf16[1664,4096]{1,0:T(8,128)(2,1)S(1)}, bf16[4096,1664]{1,0:T(8,128)(2,1)S(1)}) custom-call(bf16[4096,1664]{1,0:T(8,128)(2,1)} %hbm_ref.1, bf16[4096,1664]{1,0:T(8,128)(2,1)} %refs_5_.1), custom_call_target="tpu_custom_call" | custom-call | bytes 13631488 | tf_op jit(solution)/shard_map/load_turned/pallas_call | solution.py:58
  15.8 0.0 collective-permute-done.3.refs_3_
  15.8 0.0 collective-permute-done.1.refs_2_
  15.8 0.0 collective-permute-done.refs_1_
  15.8 0.0 collective-permute-done.2.refs_3_
  15.8 0.0 copy-done
  15.8 5.0 %forward.1 = (f32[32,3328]{1,0:T(8,128)S(1)}, bf16[32,3328]{1,0:T(8,128)(2,1)S(1)}, bf16[4096,1664]{1,0:T(8,128)(2,1)S(1)}) custom-call(bf16[16,4096]{1,0:T(8,128)(2,1)S(1)} %copy-done, bf16[16,4096]{1,0:T(8,128)(2,1)S(1)} %collective-permute-done.refs_1_, bf16[16,4096]{1,0:T(8,128)(2,1)S(1)} %collective-permute-done.1.refs_2_, ...), custom_call_target="tpu_custom_call", output_to_operand_aliasing={{2}: (6, {})} | custom-call | tf_op jit(solution)/shard_map/forward/pallas_call | solution.py:135
  20.8 0.1 collective-permute-start.4
  20.9 1.5 %collective-permute-done.4 = bf16[32,3328]{1,0:T(8,128)(2,1)S(1)} collective-permute-done((bf16[32,3328]{1,0:T(8,128)(2,1)S(1)}, bf16[32,3328]{1,0:T(8,128)(2,1)S(1)}, u32[]{:S(2)}, u32[]{:S(2)}) %collective-permute-start.4) | collective-permute-done | bytes 213024 | tf_op jit(solution)/shard_map/ppermute | solution.py:25
  22.4 0.0 copy-start.1
  22.4 1.2 %collective-permute-start.5 = (bf16[32,3328]{1,0:T(8,128)(2,1)S(1)}, bf16[32,3328]{1,0:T(8,128)(2,1)S(1)}, u32[]{:S(2)}, u32[]{:S(2)}) collective-permute-start(bf16[32,3328]{1,0:T(8,128)(2,1)S(1)} %get-tuple-element.38), channel_id=1, source_target_pairs={{0,2},{2,0},{1,3},{3,1},{4,6},{6,4},{5,7},{7,5},{8,10},{10,8},{9,1... | collective-permute-start | bytes 638984 | tf_op jit(solution)/shard_map/ppermute | solution.py:25
  23.6 4.2 %turn.1.up_ref = bf16[1664,4096]{1,0:T(8,128)(2,1)S(1)} custom-call(bf16[4096,1664]{1,0:T(8,128)(2,1)S(1)} %get-tuple-element.39.weight_ref), custom_call_target="tpu_custom_call" | custom-call | bytes 27262976 | tf_op jit(solution)/shard_map/turn/pallas_call | solution.py:86
  27.9 1.9 %collective-permute-done.5.refs_1_ = bf16[32,3328]{1,0:T(8,128)(2,1)S(1)} collective-permute-done((bf16[32,3328]{1,0:T(8,128)(2,1)S(1)}, bf16[32,3328]{1,0:T(8,128)(2,1)S(1)}, u32[]{:S(2)}, u32[]{:S(2)}) %collective-permute-start.5) | collective-permute-done | bytes 213024 | tf_op jit(solution)/shard_map/ppermute | solution.py:25
  29.7 0.0 copy-done.1
  29.7 0.2 activate.1
  29.9 0.1 collective-permute-start.6
  30.0 0.6 %copy.8 = bf16[16,1664]{1,0:T(8,128)(2,1)} copy(bf16[16,1664]{1,0:T(8,128)(2,1)S(1)} %get-tuple-element.56) | data formatting | bytes 106496
  30.6 0.8 %collective-permute-done.6.other_ref = bf16[32,3328]{1,0:T(8,128)(2,1)S(1)} collective-permute-done((bf16[32,3328]{1,0:T(8,128)(2,1)S(1)}, bf16[32,3328]{1,0:T(8,128)(2,1)S(1)}, u32[]{:S(2)}, u32[]{:S(2)}) %collective-permute-start.6) | collective-permute-done | bytes 213024 | tf_op jit(solution)/shard_map/ppermute | solution.py:25
  31.4 2.5 %backward.3 = (f32[16,2048]{1,0:T(8,128)S(1)}, bf16[16,2048]{1,0:T(8,128)(2,1)S(1)}, bf16[16,2048]{1,0:T(8,128)(2,1)S(1)}, bf16[16,2048]{1,0:T(8,128)(2,1)S(1)}) custom-call(bf16[32,3328]{1,0:T(8,128)(2,1)S(1)} %get-tuple-element.44.own_ref, bf16[32,3328]{1,0:T(8,128)(2,1)S(1)} %collective-permute-done.6.other_ref, ...), custom_call_target="tpu_custom_call" | custom-call | flops 872415232 | bytes 13631488 | tf_op jit(solution)/shard_map/backward/pallas_call | solution.py:225
  33.9 3.2 %collective-permute-start.10 = (bf16[16,2048]{1,0:T(8,128)(2,1)S(1)}, bf16[16,2048]{1,0:T(8,128)(2,1)S(1)}, u32[]{:S(2)}, u32[]{:S(2)}) collective-permute-start(bf16[16,2048]{1,0:T(8,128)(2,1)S(1)} %get-tuple-element.51), channel_id=1, source_target_pairs={{0,12},{4,8},{8,4},{12,0},{1,13},{5,9},{9,5},{13,1},{2,14},{6,10},... | collective-permute-start | bytes 196616 | tf_op jit(solution)/shard_map/ppermute | solution.py:25
  37.2 1.1 %collective-permute-start.11 = (bf16[16,2048]{1,0:T(8,128)(2,1)S(1)}, bf16[16,2048]{1,0:T(8,128)(2,1)S(1)}, u32[]{:S(2)}, u32[]{:S(2)}) collective-permute-start(bf16[16,2048]{1,0:T(8,128)(2,1)S(1)} %get-tuple-element.52), channel_id=1, source_target_pairs={{0,4},{4,0},{8,12},{12,8},{1,5},{5,1},{9,13},{13,9},{2,6},{6,2},{1... | collective-permute-start | bytes 196616 | tf_op jit(solution)/shard_map/ppermute | solution.py:25
  38.3 0.1 collective-permute-start.12
  38.4 2.5 %backward.2 = (f32[16,2048]{1,0:T(8,128)S(1)}, bf16[16,2048]{1,0:T(8,128)(2,1)S(1)}, bf16[16,2048]{1,0:T(8,128)(2,1)S(1)}, bf16[16,2048]{1,0:T(8,128)(2,1)S(1)}) custom-call(bf16[32,3328]{1,0:T(8,128)(2,1)S(1)} %get-tuple-element.44.own_ref, bf16[32,3328]{1,0:T(8,128)(2,1)S(1)} %collective-permute-done.6.other_ref, ...), custom_call_target="tpu_custom_call" | custom-call | flops 872415232 | bytes 13631488 | tf_op jit(solution)/shard_map/backward/pallas_call | solution.py:225
  40.9 3.2 %collective-permute-start.7 = (bf16[16,2048]{1,0:T(8,128)(2,1)S(1)}, bf16[16,2048]{1,0:T(8,128)(2,1)S(1)}, u32[]{:S(2)}, u32[]{:S(2)}) collective-permute-start(bf16[16,2048]{1,0:T(8,128)(2,1)S(1)} %get-tuple-element.47), channel_id=1, source_target_pairs={{0,12},{4,8},{8,4},{12,0},{1,13},{5,9},{9,5},{13,1},{2,14},{6,10},... | collective-permute-start | bytes 196616 | tf_op jit(solution)/shard_map/ppermute | solution.py:25
  44.1 0.3 collective-permute-start.8
  44.4 0.0 collective-permute-done.10
  44.4 1.0 %collective-permute-start.9 = (bf16[16,2048]{1,0:T(8,128)(2,1)S(1)}, bf16[16,2048]{1,0:T(8,128)(2,1)S(1)}, u32[]{:S(2)}, u32[]{:S(2)}) collective-permute-start(bf16[16,2048]{1,0:T(8,128)(2,1)S(1)} %get-tuple-element.49), channel_id=1, source_target_pairs={{0,8},{4,12},{8,0},{12,4},{1,9},{5,13},{9,1},{13,5},{2,10},{6,14},... | collective-permute-start | bytes 196616 | tf_op jit(solution)/shard_map/ppermute | solution.py:25
  45.4 0.0 collective-permute-done.11
  45.4 0.0 collective-permute-done.12
  45.4 1.8 %collective-permute-done.7 = bf16[16,2048]{1,0:T(8,128)(2,1)S(1)} collective-permute-done((bf16[16,2048]{1,0:T(8,128)(2,1)S(1)}, bf16[16,2048]{1,0:T(8,128)(2,1)S(1)}, u32[]{:S(2)}, u32[]{:S(2)}) %collective-permute-start.7) | collective-permute-done | bytes 65568 | tf_op jit(solution)/shard_map/ppermute | solution.py:25
  47.2 1.4 %collective-permute-done.8 = bf16[16,2048]{1,0:T(8,128)(2,1)S(1)} collective-permute-done((bf16[16,2048]{1,0:T(8,128)(2,1)S(1)}, bf16[16,2048]{1,0:T(8,128)(2,1)S(1)}, u32[]{:S(2)}, u32[]{:S(2)}) %collective-permute-start.8) | collective-permute-done | bytes 65568 | tf_op jit(solution)/shard_map/ppermute | solution.py:25
  48.5 1.0 %collective-permute-done.9 = bf16[16,2048]{1,0:T(8,128)(2,1)S(1)} collective-permute-done((bf16[16,2048]{1,0:T(8,128)(2,1)S(1)}, bf16[16,2048]{1,0:T(8,128)(2,1)S(1)}, u32[]{:S(2)}, u32[]{:S(2)}) %collective-permute-start.9) | collective-permute-done | bytes 65568 | tf_op jit(solution)/shard_map/ppermute | solution.py:25
  49.6 0.7 %pad_maximum_fusion = bf16[16,4096]{1,0:T(8,128)(2,1)} fusion(bf16[16,2048]{1,0:T(8,128)(2,1)S(1)} %add_convert_fusion, bf16[16,2048]{1,0:T(8,128)(2,1)S(1)} %add_convert_fusion.1), kind=kLoop, calls=%fused_computation.1 | loop fusion | flops 262144 | bytes 262144 | tf_op jit(solution)/shard_map/concatenate | solution.py:279
  (3 shorter events, 0.1 us)
Async XLA Ops:
  0.6 15.2 %copy-start = (bf16[16,4096]{1,0:T(8,128)(2,1)S(1)}, bf16[16,4096]{1,0:T(8,128)(2,1)}, u32[]{:S(2)}) copy-start(bf16[16,4096]{1,0:T(8,128)(2,1)} %refs_0_) | copy-start | bytes 393220
  0.6 15.1 %collective-permute-start.1 = (bf16[16,4096]{1,0:T(8,128)(2,1)}, bf16[16,4096]{1,0:T(8,128)(2,1)S(1)}, u32[]{:S(2)}, u32[]{:S(2)}) collective-permute-start(bf16[16,4096]{1,0:T(8,128)(2,1)} %refs_0_), channel_id=1, source_target_pairs={{0,8},{4,12},{8,0},{12,4},{1,9},{5,13},{9,1},{13,5},{2,10},{6,14},... | collective-permute-start | bytes 393224 | tf_op jit(solution)/shard_map/ppermute | solution.py:25
  4.7 11.1 %collective-permute-start = (bf16[16,4096]{1,0:T(8,128)(2,1)}, bf16[16,4096]{1,0:T(8,128)(2,1)S(1)}, u32[]{:S(2)}, u32[]{:S(2)}) collective-permute-start(bf16[16,4096]{1,0:T(8,128)(2,1)} %refs_0_), channel_id=1, source_target_pairs={{0,12},{4,8},{8,4},{12,0},{1,13},{5,9},{9,5},{13,1},{2,14},{6,10},... | collective-permute-start | bytes 393224 | tf_op jit(solution)/shard_map/ppermute | solution.py:25
  6.1 9.7 %collective-permute-start.2 = (bf16[16,4096]{1,0:T(8,128)(2,1)}, bf16[16,4096]{1,0:T(8,128)(2,1)S(1)}, u32[]{:S(2)}, u32[]{:S(2)}) collective-permute-start(bf16[16,4096]{1,0:T(8,128)(2,1)} %refs_0_), channel_id=1, source_target_pairs={{0,4},{4,0},{8,12},{12,8},{1,5},{5,1},{9,13},{13,9},{2,6},{6,2},{1... | collective-permute-start | bytes 393224 | tf_op jit(solution)/shard_map/ppermute | solution.py:25
  6.3 9.5 %collective-permute-start.3 = (bf16[16,1664]{1,0:T(8,128)(2,1)}, bf16[16,1664]{1,0:T(8,128)(2,1)S(1)}, u32[]{:S(2)}, u32[]{:S(2)}) collective-permute-start(bf16[16,1664]{1,0:T(8,128)(2,1)} %refs_2_), channel_id=1, source_target_pairs={{0,2},{2,0},{1,3},{3,1},{4,6},{6,4},{5,7},{7,5},{8,10},{10,8},{9,1... | collective-permute-start | bytes 159752 | tf_op jit(solution)/shard_map/ppermute | solution.py:25
  20.8 1.5 %collective-permute-start.4 = (bf16[32,3328]{1,0:T(8,128)(2,1)S(1)}, bf16[32,3328]{1,0:T(8,128)(2,1)S(1)}, u32[]{:S(2)}, u32[]{:S(2)}) collective-permute-start(bf16[32,3328]{1,0:T(8,128)(2,1)S(1)} %get-tuple-element.36), channel_id=1, source_target_pairs={{0,1},{1,0},{2,3},{3,2},{4,5},{5,4},{6,7},{7,6},{8,9},{9,8},{10,11... | collective-permute-start | bytes 638984 | tf_op jit(solution)/shard_map/ppermute | solution.py:25
  22.4 7.4 %copy-start.1 = (bf16[16,1664]{1,0:T(8,128)(2,1)S(1)}, bf16[16,1664]{1,0:T(8,128)(2,1)}, u32[]{:S(2)}) copy-start(bf16[16,1664]{1,0:T(8,128)(2,1)} %refs_2_) | copy-start | bytes 159748
  22.4 7.4 %collective-permute-start.5 = (bf16[32,3328]{1,0:T(8,128)(2,1)S(1)}, bf16[32,3328]{1,0:T(8,128)(2,1)S(1)}, u32[]{:S(2)}, u32[]{:S(2)}) collective-permute-start(bf16[32,3328]{1,0:T(8,128)(2,1)S(1)} %get-tuple-element.38), channel_id=1, source_target_pairs={{0,2},{2,0},{1,3},{3,1},{4,6},{6,4},{5,7},{7,5},{8,10},{10,8},{9,1... | collective-permute-start | bytes 638984 | tf_op jit(solution)/shard_map/ppermute | solution.py:25
  29.9 1.5 %collective-permute-start.6 = (bf16[32,3328]{1,0:T(8,128)(2,1)S(1)}, bf16[32,3328]{1,0:T(8,128)(2,1)S(1)}, u32[]{:S(2)}, u32[]{:S(2)}) collective-permute-start(bf16[32,3328]{1,0:T(8,128)(2,1)S(1)} %get-tuple-element.44.own_ref), channel_id=1, source_target_pairs={{0,1},{1,0},{2,3},{3,2},{4,5},{5,4},{6,7},{7,6},{8,9},{9,8},{10,11... | collective-permute-start | bytes 638984 | tf_op jit(solution)/shard_map/ppermute | solution.py:25
  33.9 10.4 %collective-permute-start.10 = (bf16[16,2048]{1,0:T(8,128)(2,1)S(1)}, bf16[16,2048]{1,0:T(8,128)(2,1)S(1)}, u32[]{:S(2)}, u32[]{:S(2)}) collective-permute-start(bf16[16,2048]{1,0:T(8,128)(2,1)S(1)} %get-tuple-element.51), channel_id=1, source_target_pairs={{0,12},{4,8},{8,4},{12,0},{1,13},{5,9},{9,5},{13,1},{2,14},{6,10},... | collective-permute-start | bytes 196616 | tf_op jit(solution)/shard_map/ppermute | solution.py:25
  37.2 8.2 %collective-permute-start.11 = (bf16[16,2048]{1,0:T(8,128)(2,1)S(1)}, bf16[16,2048]{1,0:T(8,128)(2,1)S(1)}, u32[]{:S(2)}, u32[]{:S(2)}) collective-permute-start(bf16[16,2048]{1,0:T(8,128)(2,1)S(1)} %get-tuple-element.52), channel_id=1, source_target_pairs={{0,4},{4,0},{8,12},{12,8},{1,5},{5,1},{9,13},{13,9},{2,6},{6,2},{1... | collective-permute-start | bytes 196616 | tf_op jit(solution)/shard_map/ppermute | solution.py:25
  38.3 7.1 %collective-permute-start.12 = (bf16[16,2048]{1,0:T(8,128)(2,1)S(1)}, bf16[16,2048]{1,0:T(8,128)(2,1)S(1)}, u32[]{:S(2)}, u32[]{:S(2)}) collective-permute-start(bf16[16,2048]{1,0:T(8,128)(2,1)S(1)} %get-tuple-element.53), channel_id=1, source_target_pairs={{0,8},{4,12},{8,0},{12,4},{1,9},{5,13},{9,1},{13,5},{2,10},{6,14},... | collective-permute-start | bytes 196616 | tf_op jit(solution)/shard_map/ppermute | solution.py:25
  40.9 6.3 %collective-permute-start.7 = (bf16[16,2048]{1,0:T(8,128)(2,1)S(1)}, bf16[16,2048]{1,0:T(8,128)(2,1)S(1)}, u32[]{:S(2)}, u32[]{:S(2)}) collective-permute-start(bf16[16,2048]{1,0:T(8,128)(2,1)S(1)} %get-tuple-element.47), channel_id=1, source_target_pairs={{0,12},{4,8},{8,4},{12,0},{1,13},{5,9},{9,5},{13,1},{2,14},{6,10},... | collective-permute-start | bytes 196616 | tf_op jit(solution)/shard_map/ppermute | solution.py:25
  44.1 4.4 %collective-permute-start.8 = (bf16[16,2048]{1,0:T(8,128)(2,1)S(1)}, bf16[16,2048]{1,0:T(8,128)(2,1)S(1)}, u32[]{:S(2)}, u32[]{:S(2)}) collective-permute-start(bf16[16,2048]{1,0:T(8,128)(2,1)S(1)} %get-tuple-element.48), channel_id=1, source_target_pairs={{0,4},{4,0},{8,12},{12,8},{1,5},{5,1},{9,13},{13,9},{2,6},{6,2},{1... | collective-permute-start | bytes 196616 | tf_op jit(solution)/shard_map/ppermute | solution.py:25
  44.4 5.2 %collective-permute-start.9 = (bf16[16,2048]{1,0:T(8,128)(2,1)S(1)}, bf16[16,2048]{1,0:T(8,128)(2,1)S(1)}, u32[]{:S(2)}, u32[]{:S(2)}) collective-permute-start(bf16[16,2048]{1,0:T(8,128)(2,1)S(1)} %get-tuple-element.49), channel_id=1, source_target_pairs={{0,8},{4,12},{8,0},{12,4},{1,9},{5,13},{9,1},{13,5},{2,10},{6,14},... | collective-permute-start | bytes 196616 | tf_op jit(solution)/shard_map/ppermute | solution.py:25

commit v4 on v3

--- a/solution.py
+++ b/solution.py
@@ -10,7 +10,7 @@
 
 VMEM = pl.BlockSpec(memory_space=pltpu.VMEM)
 PARAMS = pltpu.CompilerParams(vmem_limit_bytes=8 << 20)
-NT = (((1,), (1,)), ((), ()))
+PARTS = 2
 
 
 def partner(index, step, size):
@@ -23,10 +23,6 @@
 
 def exchange(x, axis, step, size):
     return lax.ppermute(x, axis, [(i, partner(i, step, size)) for i in range(size)])
-
-
-def tiles(width, tile=256):
-    return width // tile, width // tile * tile
 
 
 def load_turned(weight, next_weight, step=512):
@@ -68,7 +64,7 @@
 
 
 def ahead_rows(depth):
-    return depth * AHEAD // 4
+    return depth * 3 // 4
 
 
 def turn(weight, step=512):
@@ -120,8 +116,8 @@
                 x_ref[pl.ds(pl.multiple_of(place, piece), piece), :] = block[pl.ds(i * piece, piece), :]
 
         def columns(weight, out):
-            for begin in range(0, hidden_cols, 256):
-                width = min(256, hidden_cols - begin)
+            for begin in range(0, hidden_cols, 512):
+                width = min(512, hidden_cols - begin)
                 product = jnp.dot(x_ref[...], weight[:, begin : begin + width], preferred_element_type=jnp.float32)
                 cols = pl.ds(out + begin, width)
                 keep_ref[:, cols] = product[:half]
@@ -136,7 +132,7 @@
         kernel,
         out_shape=[
             jax.ShapeDtypeStruct(shape, jnp.float32),
-            jax.ShapeDtypeStruct(shape, SUB_DTYPE),
+            jax.ShapeDtypeStruct(shape, jnp.bfloat16),
             pltpu.VMEM((depth, hidden_cols), jnp.bfloat16),
         ],
         in_specs=[VMEM] * (wide + 1) + [pl.BlockSpec(memory_space=pltpu.HBM), VMEM, VMEM],
@@ -238,7 +234,7 @@
 
 def shards(tokens, gate_weight, up_weight, hidden_grad, sizes):
     wide, narrow, sub = sizes
-    order = list(AG_ORDER) if wide == 4 else list(range(1, wide))
+    order = [3, 2, 1] if wide == 4 else list(range(1, wide))
     got = {step: exchange(tokens, "wide", step, wide) for step in order}
     steps = [0] + order
     blocks = [tokens] + [got[step] for step in order]
@@ -257,35 +253,19 @@
     hidden, pre = activate(chip, others, grads, sizes)
     pre_other = exchange(pre, "sub", 1, sub)
 
-    order = list(RS_ORDER) if wide == 4 else list(range(1, wide))
+    order = list(range(1, wide))
     f32, bf16 = jnp.float32, jnp.bfloat16
     bwd = functools.partial(backward, pre, pre_other, gate_turned, up_turned, sizes=sizes)
     direct = [((0,), f32)] + [((step,), bf16) for step in order]
-    depth = tokens.shape[1]
-    widths = [depth * share // sum(SHARES) for share in SHARES]
-    begins = [sum(widths[:i]) for i in range(len(widths))]
-    totals, owns, sends = [], [], []
-    for begin, width in zip(begins, widths):
-        own, *send = bwd(begin=begin, depth=width, groups=direct)
-        owns.append(own)
-        sends.append(dict(zip(order, send)))
-    whole = {}
-    if MERGE:
-        whole[1] = exchange(jnp.concatenate([send.pop(1) for send in sends], axis=1), "wide", 1, wide)
-    got = [{step: exchange(x, "wide", step, wide) for step, x in send.items()} for send in sends]
-    for begin, width, own, parts in zip(begins, widths, owns, got):
-        parts.update({step: x[:, begin : begin + width] for step, x in whole.items()})
-        totals.append(own + sum(x.astype(f32) for x in parts.values()))
+    width = tokens.shape[1] // PARTS
+    totals = []
+    for part in range(PARTS):
+        own, *sends = bwd(begin=part * width, depth=width, groups=direct)
+        sends = dict(zip(order, sends))
+        turns = [3, 1, 2] if wide == 4 else order
+        got = [exchange(sends[step], "wide", step, wide) for step in turns]
+        totals.append(own + sum(x.astype(f32) for x in got))
     return (hidden, jnp.concatenate([total.astype(bf16) for total in totals], axis=1))
-
-
-SUB_DTYPE = jnp.bfloat16
-AHEAD = 3
-SHARES = (1, 1)
-AG_ORDER = (3, 2, 1)
-RS_ORDER = (3, 1, 2)
-RELAY = False
-MERGE = False
 
 
 def solution(mesh):

time: 50.4 us -> 50.4 us (level)
  no operation moved by 1% of the time
where the time goes in v4:
time: 50.4 us; the launch traced here: 50.2 us
  Pallas kernels  22.3 us (44%)
  starting transfers between devices  17.4 us (35%)
  waiting for transfers between devices  8.31 us (16%)
  other arithmetic  0.78 us (2%)
  between operations  0.76 us (2%)
  local copies, waits for them, and re-layouts  0.63 us (1%)
    ppermute x13, starting transfers between devices, exchange(): lax.ppermute(x, axis, [(i, partner(i, step, size)) for i in range(size)])  17.4 us
    ppermute x13, waiting for transfers between devices, exchange(): lax.ppermute(x, axis, [(i, partner(i, step, size)) for i in range(size)])  8.31 us
    pallas_call x1, Pallas kernels, load_turned(): pl.pallas_call(kernel, out_shape=[shape, pltpu.VMEM((hidden_cols, depth),...  7.95 us
    pallas_call x2, Pallas kernels, backward(): pl.pallas_call(kernel, out_shape=[jax.ShapeDtypeStruct((len(steps) * bloc...  5.01 us
    pallas_call x1, Pallas kernels, forward(): pl.pallas_call(kernel, out_shape=[jax.ShapeDtypeStruct(shape, jnp.float32...  4.95 us
    pallas_call x1, Pallas kernels, turn(): pl.pallas_call(kernel, out_shape=pltpu.VMEM((hidden_cols, depth), jnp.bfl...  4.24 us
  transfers between devices with their start and end apart: 13, of which 6 were waited for; matrix products, arithmetic and copies ran while one was open for 1% of the time, Pallas kernels for 29%

profile of v4, /device:TPU:0, one launch (start us, length us, event | category | flops | bytes accessed | tf_op | source)
XLA Modules:
  0.0 50.2 jit_solution(4433546578061297510)
XLA Ops:
  0.6 0.0 copy-start
  0.6 4.1 %collective-permute-start.1 = (bf16[16,4096]{1,0:T(8,128)(2,1)}, bf16[16,4096]{1,0:T(8,128)(2,1)S(1)}, u32[]{:S(2)}, u32[]{:S(2)}) collective-permute-start(bf16[16,4096]{1,0:T(8,128)(2,1)} %refs_0_), channel_id=1, source_target_pairs={{0,8},{4,12},{8,0},{12,4},{1,9},{5,13},{9,1},{13,5},{2,10},{6,14},... | collective-permute-start | bytes 393224 | tf_op jit(solution)/shard_map/ppermute | solution.py:25
  4.7 1.3 %collective-permute-start = (bf16[16,4096]{1,0:T(8,128)(2,1)}, bf16[16,4096]{1,0:T(8,128)(2,1)S(1)}, u32[]{:S(2)}, u32[]{:S(2)}) collective-permute-start(bf16[16,4096]{1,0:T(8,128)(2,1)} %refs_0_), channel_id=1, source_target_pairs={{0,12},{4,8},{8,4},{12,0},{1,13},{5,9},{9,5},{13,1},{2,14},{6,10},... | collective-permute-start | bytes 393224 | tf_op jit(solution)/shard_map/ppermute | solution.py:25
  6.1 0.2 collective-permute-start.2
  6.3 1.5 %collective-permute-start.3 = (bf16[16,1664]{1,0:T(8,128)(2,1)}, bf16[16,1664]{1,0:T(8,128)(2,1)S(1)}, u32[]{:S(2)}, u32[]{:S(2)}) collective-permute-start(bf16[16,1664]{1,0:T(8,128)(2,1)} %refs_2_), channel_id=1, source_target_pairs={{0,2},{2,0},{1,3},{3,1},{4,6},{6,4},{5,7},{7,5},{8,10},{10,8},{9,1... | collective-permute-start | bytes 159752 | tf_op jit(solution)/shard_map/ppermute | solution.py:25
  7.8 8.0 %load_turned.1 = (bf16[4096,1664]{1,0:T(8,128)(2,1)S(1)}, bf16[1664,4096]{1,0:T(8,128)(2,1)S(1)}, bf16[4096,1664]{1,0:T(8,128)(2,1)S(1)}) custom-call(bf16[4096,1664]{1,0:T(8,128)(2,1)} %hbm_ref.1, bf16[4096,1664]{1,0:T(8,128)(2,1)} %refs_5_.1), custom_call_target="tpu_custom_call" | custom-call | bytes 13631488 | tf_op jit(solution)/shard_map/load_turned/pallas_call | solution.py:54
  15.8 0.0 collective-permute-done.3.refs_3_
  15.8 0.0 collective-permute-done.1.refs_2_
  15.8 0.0 collective-permute-done.refs_1_
  15.8 0.0 collective-permute-done.2.refs_3_
  15.8 0.0 copy-done
  15.8 5.0 %forward.1 = (f32[32,3328]{1,0:T(8,128)S(1)}, bf16[32,3328]{1,0:T(8,128)(2,1)S(1)}, bf16[4096,1664]{1,0:T(8,128)(2,1)S(1)}) custom-call(bf16[16,4096]{1,0:T(8,128)(2,1)S(1)} %copy-done, bf16[16,4096]{1,0:T(8,128)(2,1)S(1)} %collective-permute-done.refs_1_, bf16[16,4096]{1,0:T(8,128)(2,1)S(1)} %collective-permute-done.1.refs_2_, ...), custom_call_target="tpu_custom_call", output_to_operand_aliasing={{2}: (6, {})} | custom-call | tf_op jit(solution)/shard_map/forward/pallas_call | solution.py:131
  20.8 0.1 collective-permute-start.4
  20.9 1.5 %collective-permute-done.4 = bf16[32,3328]{1,0:T(8,128)(2,1)S(1)} collective-permute-done((bf16[32,3328]{1,0:T(8,128)(2,1)S(1)}, bf16[32,3328]{1,0:T(8,128)(2,1)S(1)}, u32[]{:S(2)}, u32[]{:S(2)}) %collective-permute-start.4) | collective-permute-done | bytes 213024 | tf_op jit(solution)/shard_map/ppermute | solution.py:25
  22.4 0.0 copy-start.1
  22.4 1.2 %collective-permute-start.5 = (bf16[32,3328]{1,0:T(8,128)(2,1)S(1)}, bf16[32,3328]{1,0:T(8,128)(2,1)S(1)}, u32[]{:S(2)}, u32[]{:S(2)}) collective-permute-start(bf16[32,3328]{1,0:T(8,128)(2,1)S(1)} %get-tuple-element.38), channel_id=1, source_target_pairs={{0,2},{2,0},{1,3},{3,1},{4,6},{6,4},{5,7},{7,5},{8,10},{10,8},{9,1... | collective-permute-start | bytes 638984 | tf_op jit(solution)/shard_map/ppermute | solution.py:25
  23.6 4.2 %turn.1.up_ref = bf16[1664,4096]{1,0:T(8,128)(2,1)S(1)} custom-call(bf16[4096,1664]{1,0:T(8,128)(2,1)S(1)} %get-tuple-element.39.weight_ref), custom_call_target="tpu_custom_call" | custom-call | bytes 27262976 | tf_op jit(solution)/shard_map/turn/pallas_call | solution.py:82
  27.9 1.9 %collective-permute-done.5.refs_1_ = bf16[32,3328]{1,0:T(8,128)(2,1)S(1)} collective-permute-done((bf16[32,3328]{1,0:T(8,128)(2,1)S(1)}, bf16[32,3328]{1,0:T(8,128)(2,1)S(1)}, u32[]{:S(2)}, u32[]{:S(2)}) %collective-permute-start.5) | collective-permute-done | bytes 213024 | tf_op jit(solution)/shard_map/ppermute | solution.py:25
  29.7 0.0 copy-done.1
  29.7 0.2 activate.1
  29.9 0.1 collective-permute-start.6
  30.0 0.6 %copy.8 = bf16[16,1664]{1,0:T(8,128)(2,1)} copy(bf16[16,1664]{1,0:T(8,128)(2,1)S(1)} %get-tuple-element.56) | data formatting | bytes 106496
  30.6 0.8 %collective-permute-done.6.other_ref = bf16[32,3328]{1,0:T(8,128)(2,1)S(1)} collective-permute-done((bf16[32,3328]{1,0:T(8,128)(2,1)S(1)}, bf16[32,3328]{1,0:T(8,128)(2,1)S(1)}, u32[]{:S(2)}, u32[]{:S(2)}) %collective-permute-start.6) | collective-permute-done | bytes 213024 | tf_op jit(solution)/shard_map/ppermute | solution.py:25
  31.4 2.5 %backward.3 = (f32[16,2048]{1,0:T(8,128)S(1)}, bf16[16,2048]{1,0:T(8,128)(2,1)S(1)}, bf16[16,2048]{1,0:T(8,128)(2,1)S(1)}, bf16[16,2048]{1,0:T(8,128)(2,1)S(1)}) custom-call(bf16[32,3328]{1,0:T(8,128)(2,1)S(1)} %get-tuple-element.44.own_ref, bf16[32,3328]{1,0:T(8,128)(2,1)S(1)} %collective-permute-done.6.other_ref, ...), custom_call_target="tpu_custom_call" | custom-call | flops 872415232 | bytes 13631488 | tf_op jit(solution)/shard_map/backward/pallas_call | solution.py:221
  33.9 3.2 %collective-permute-start.10 = (bf16[16,2048]{1,0:T(8,128)(2,1)S(1)}, bf16[16,2048]{1,0:T(8,128)(2,1)S(1)}, u32[]{:S(2)}, u32[]{:S(2)}) collective-permute-start(bf16[16,2048]{1,0:T(8,128)(2,1)S(1)} %get-tuple-element.51), channel_id=1, source_target_pairs={{0,12},{4,8},{8,4},{12,0},{1,13},{5,9},{9,5},{13,1},{2,14},{6,10},... | collective-permute-start | bytes 196616 | tf_op jit(solution)/shard_map/ppermute | solution.py:25
  37.2 1.1 %collective-permute-start.11 = (bf16[16,2048]{1,0:T(8,128)(2,1)S(1)}, bf16[16,2048]{1,0:T(8,128)(2,1)S(1)}, u32[]{:S(2)}, u32[]{:S(2)}) collective-permute-start(bf16[16,2048]{1,0:T(8,128)(2,1)S(1)} %get-tuple-element.52), channel_id=1, source_target_pairs={{0,4},{4,0},{8,12},{12,8},{1,5},{5,1},{9,13},{13,9},{2,6},{6,2},{1... | collective-permute-start | bytes 196616 | tf_op jit(solution)/shard_map/ppermute | solution.py:25
  38.3 0.1 collective-permute-start.12
  38.4 2.5 %backward.2 = (f32[16,2048]{1,0:T(8,128)S(1)}, bf16[16,2048]{1,0:T(8,128)(2,1)S(1)}, bf16[16,2048]{1,0:T(8,128)(2,1)S(1)}, bf16[16,2048]{1,0:T(8,128)(2,1)S(1)}) custom-call(bf16[32,3328]{1,0:T(8,128)(2,1)S(1)} %get-tuple-element.44.own_ref, bf16[32,3328]{1,0:T(8,128)(2,1)S(1)} %collective-permute-done.6.other_ref, ...), custom_call_target="tpu_custom_call" | custom-call | flops 872415232 | bytes 13631488 | tf_op jit(solution)/shard_map/backward/pallas_call | solution.py:221
  40.9 3.2 %collective-permute-start.7 = (bf16[16,2048]{1,0:T(8,128)(2,1)S(1)}, bf16[16,2048]{1,0:T(8,128)(2,1)S(1)}, u32[]{:S(2)}, u32[]{:S(2)}) collective-permute-start(bf16[16,2048]{1,0:T(8,128)(2,1)S(1)} %get-tuple-element.47), channel_id=1, source_target_pairs={{0,12},{4,8},{8,4},{12,0},{1,13},{5,9},{9,5},{13,1},{2,14},{6,10},... | collective-permute-start | bytes 196616 | tf_op jit(solution)/shard_map/ppermute | solution.py:25
  44.1 0.3 collective-permute-start.8
  44.4 0.0 collective-permute-done.10
  44.4 1.0 %collective-permute-start.9 = (bf16[16,2048]{1,0:T(8,128)(2,1)S(1)}, bf16[16,2048]{1,0:T(8,128)(2,1)S(1)}, u32[]{:S(2)}, u32[]{:S(2)}) collective-permute-start(bf16[16,2048]{1,0:T(8,128)(2,1)S(1)} %get-tuple-element.49), channel_id=1, source_target_pairs={{0,8},{4,12},{8,0},{12,4},{1,9},{5,13},{9,1},{13,5},{2,10},{6,14},... | collective-permute-start | bytes 196616 | tf_op jit(solution)/shard_map/ppermute | solution.py:25
  45.4 0.0 collective-permute-done.11
  45.4 0.0 collective-permute-done.12
  45.4 1.8 %collective-permute-done.7 = bf16[16,2048]{1,0:T(8,128)(2,1)S(1)} collective-permute-done((bf16[16,2048]{1,0:T(8,128)(2,1)S(1)}, bf16[16,2048]{1,0:T(8,128)(2,1)S(1)}, u32[]{:S(2)}, u32[]{:S(2)}) %collective-permute-start.7) | collective-permute-done | bytes 65568 | tf_op jit(solution)/shard_map/ppermute | solution.py:25
  47.2 1.4 %collective-permute-done.8 = bf16[16,2048]{1,0:T(8,128)(2,1)S(1)} collective-permute-done((bf16[16,2048]{1,0:T(8,128)(2,1)S(1)}, bf16[16,2048]{1,0:T(8,128)(2,1)S(1)}, u32[]{:S(2)}, u32[]{:S(2)}) %collective-permute-start.8) | collective-permute-done | bytes 65568 | tf_op jit(solution)/shard_map/ppermute | solution.py:25
  48.5 1.0 %collective-permute-done.9 = bf16[16,2048]{1,0:T(8,128)(2,1)S(1)} collective-permute-done((bf16[16,2048]{1,0:T(8,128)(2,1)S(1)}, bf16[16,2048]{1,0:T(8,128)(2,1)S(1)}, u32[]{:S(2)}, u32[]{:S(2)}) %collective-permute-start.9) | collective-permute-done | bytes 65568 | tf_op jit(solution)/shard_map/ppermute | solution.py:25
  49.6 0.7 %pad_maximum_fusion = bf16[16,4096]{1,0:T(8,128)(2,1)} fusion(bf16[16,2048]{1,0:T(8,128)(2,1)S(1)} %add_convert_fusion, bf16[16,2048]{1,0:T(8,128)(2,1)S(1)} %add_convert_fusion.1), kind=kLoop, calls=%fused_computation.1 | loop fusion | flops 262144 | bytes 262144 | tf_op jit(solution)/shard_map/concatenate | solution.py:268
  (3 shorter events, 0.1 us)
Async XLA Ops:
  0.6 15.2 %copy-start = (bf16[16,4096]{1,0:T(8,128)(2,1)S(1)}, bf16[16,4096]{1,0:T(8,128)(2,1)}, u32[]{:S(2)}) copy-start(bf16[16,4096]{1,0:T(8,128)(2,1)} %refs_0_) | copy-start | bytes 393220
  0.6 15.1 %collective-permute-start.1 = (bf16[16,4096]{1,0:T(8,128)(2,1)}, bf16[16,4096]{1,0:T(8,128)(2,1)S(1)}, u32[]{:S(2)}, u32[]{:S(2)}) collective-permute-start(bf16[16,4096]{1,0:T(8,128)(2,1)} %refs_0_), channel_id=1, source_target_pairs={{0,8},{4,12},{8,0},{12,4},{1,9},{5,13},{9,1},{13,5},{2,10},{6,14},... | collective-permute-start | bytes 393224 | tf_op jit(solution)/shard_map/ppermute | solution.py:25
  4.7 11.1 %collective-permute-start = (bf16[16,4096]{1,0:T(8,128)(2,1)}, bf16[16,4096]{1,0:T(8,128)(2,1)S(1)}, u32[]{:S(2)}, u32[]{:S(2)}) collective-permute-start(bf16[16,4096]{1,0:T(8,128)(2,1)} %refs_0_), channel_id=1, source_target_pairs={{0,12},{4,8},{8,4},{12,0},{1,13},{5,9},{9,5},{13,1},{2,14},{6,10},... | collective-permute-start | bytes 393224 | tf_op jit(solution)/shard_map/ppermute | solution.py:25
  6.1 9.7 %collective-permute-start.2 = (bf16[16,4096]{1,0:T(8,128)(2,1)}, bf16[16,4096]{1,0:T(8,128)(2,1)S(1)}, u32[]{:S(2)}, u32[]{:S(2)}) collective-permute-start(bf16[16,4096]{1,0:T(8,128)(2,1)} %refs_0_), channel_id=1, source_target_pairs={{0,4},{4,0},{8,12},{12,8},{1,5},{5,1},{9,13},{13,9},{2,6},{6,2},{1... | collective-permute-start | bytes 393224 | tf_op jit(solution)/shard_map/ppermute | solution.py:25
  6.3 9.5 %collective-permute-start.3 = (bf16[16,1664]{1,0:T(8,128)(2,1)}, bf16[16,1664]{1,0:T(8,128)(2,1)S(1)}, u32[]{:S(2)}, u32[]{:S(2)}) collective-permute-start(bf16[16,1664]{1,0:T(8,128)(2,1)} %refs_2_), channel_id=1, source_target_pairs={{0,2},{2,0},{1,3},{3,1},{4,6},{6,4},{5,7},{7,5},{8,10},{10,8},{9,1... | collective-permute-start | bytes 159752 | tf_op jit(solution)/shard_map/ppermute | solution.py:25
  20.8 1.5 %collective-permute-start.4 = (bf16[32,3328]{1,0:T(8,128)(2,1)S(1)}, bf16[32,3328]{1,0:T(8,128)(2,1)S(1)}, u32[]{:S(2)}, u32[]{:S(2)}) collective-permute-start(bf16[32,3328]{1,0:T(8,128)(2,1)S(1)} %get-tuple-element.36), channel_id=1, source_target_pairs={{0,1},{1,0},{2,3},{3,2},{4,5},{5,4},{6,7},{7,6},{8,9},{9,8},{10,11... | collective-permute-start | bytes 638984 | tf_op jit(solution)/shard_map/ppermute | solution.py:25
  22.4 7.4 %copy-start.1 = (bf16[16,1664]{1,0:T(8,128)(2,1)S(1)}, bf16[16,1664]{1,0:T(8,128)(2,1)}, u32[]{:S(2)}) copy-start(bf16[16,1664]{1,0:T(8,128)(2,1)} %refs_2_) | copy-start | bytes 159748
  22.4 7.4 %collective-permute-start.5 = (bf16[32,3328]{1,0:T(8,128)(2,1)S(1)}, bf16[32,3328]{1,0:T(8,128)(2,1)S(1)}, u32[]{:S(2)}, u32[]{:S(2)}) collective-permute-start(bf16[32,3328]{1,0:T(8,128)(2,1)S(1)} %get-tuple-element.38), channel_id=1, source_target_pairs={{0,2},{2,0},{1,3},{3,1},{4,6},{6,4},{5,7},{7,5},{8,10},{10,8},{9,1... | collective-permute-start | bytes 638984 | tf_op jit(solution)/shard_map/ppermute | solution.py:25
  29.9 1.5 %collective-permute-start.6 = (bf16[32,3328]{1,0:T(8,128)(2,1)S(1)}, bf16[32,3328]{1,0:T(8,128)(2,1)S(1)}, u32[]{:S(2)}, u32[]{:S(2)}) collective-permute-start(bf16[32,3328]{1,0:T(8,128)(2,1)S(1)} %get-tuple-element.44.own_ref), channel_id=1, source_target_pairs={{0,1},{1,0},{2,3},{3,2},{4,5},{5,4},{6,7},{7,6},{8,9},{9,8},{10,11... | collective-permute-start | bytes 638984 | tf_op jit(solution)/shard_map/ppermute | solution.py:25
  33.9 10.4 %collective-permute-start.10 = (bf16[16,2048]{1,0:T(8,128)(2,1)S(1)}, bf16[16,2048]{1,0:T(8,128)(2,1)S(1)}, u32[]{:S(2)}, u32[]{:S(2)}) collective-permute-start(bf16[16,2048]{1,0:T(8,128)(2,1)S(1)} %get-tuple-element.51), channel_id=1, source_target_pairs={{0,12},{4,8},{8,4},{12,0},{1,13},{5,9},{9,5},{13,1},{2,14},{6,10},... | collective-permute-start | bytes 196616 | tf_op jit(solution)/shard_map/ppermute | solution.py:25
  37.2 8.2 %collective-permute-start.11 = (bf16[16,2048]{1,0:T(8,128)(2,1)S(1)}, bf16[16,2048]{1,0:T(8,128)(2,1)S(1)}, u32[]{:S(2)}, u32[]{:S(2)}) collective-permute-start(bf16[16,2048]{1,0:T(8,128)(2,1)S(1)} %get-tuple-element.52), channel_id=1, source_target_pairs={{0,4},{4,0},{8,12},{12,8},{1,5},{5,1},{9,13},{13,9},{2,6},{6,2},{1... | collective-permute-start | bytes 196616 | tf_op jit(solution)/shard_map/ppermute | solution.py:25
  38.3 7.1 %collective-permute-start.12 = (bf16[16,2048]{1,0:T(8,128)(2,1)S(1)}, bf16[16,2048]{1,0:T(8,128)(2,1)S(1)}, u32[]{:S(2)}, u32[]{:S(2)}) collective-permute-start(bf16[16,2048]{1,0:T(8,128)(2,1)S(1)} %get-tuple-element.53), channel_id=1, source_target_pairs={{0,8},{4,12},{8,0},{12,4},{1,9},{5,13},{9,1},{13,5},{2,10},{6,14},... | collective-permute-start | bytes 196616 | tf_op jit(solution)/shard_map/ppermute | solution.py:25
  40.9 6.3 %collective-permute-start.7 = (bf16[16,2048]{1,0:T(8,128)(2,1)S(1)}, bf16[16,2048]{1,0:T(8,128)(2,1)S(1)}, u32[]{:S(2)}, u32[]{:S(2)}) collective-permute-start(bf16[16,2048]{1,0:T(8,128)(2,1)S(1)} %get-tuple-element.47), channel_id=1, source_target_pairs={{0,12},{4,8},{8,4},{12,0},{1,13},{5,9},{9,5},{13,1},{2,14},{6,10},... | collective-permute-start | bytes 196616 | tf_op jit(solution)/shard_map/ppermute | solution.py:25
  44.1 4.4 %collective-permute-start.8 = (bf16[16,2048]{1,0:T(8,128)(2,1)S(1)}, bf16[16,2048]{1,0:T(8,128)(2,1)S(1)}, u32[]{:S(2)}, u32[]{:S(2)}) collective-permute-start(bf16[16,2048]{1,0:T(8,128)(2,1)S(1)} %get-tuple-element.48), channel_id=1, source_target_pairs={{0,4},{4,0},{8,12},{12,8},{1,5},{5,1},{9,13},{13,9},{2,6},{6,2},{1... | collective-permute-start | bytes 196616 | tf_op jit(solution)/shard_map/ppermute | solution.py:25
  44.4 5.2 %collective-permute-start.9 = (bf16[16,2048]{1,0:T(8,128)(2,1)S(1)}, bf16[16,2048]{1,0:T(8,128)(2,1)S(1)}, u32[]{:S(2)}, u32[]{:S(2)}) collective-permute-start(bf16[16,2048]{1,0:T(8,128)(2,1)S(1)} %get-tuple-element.49), channel_id=1, source_target_pairs={{0,8},{4,12},{8,0},{12,4},{1,9},{5,13},{9,1},{13,5},{2,10},{6,14},... | collective-permute-start | bytes 196616 | tf_op jit(solution)/shard_map/ppermute | solution.py:25

commit v5 on v4

--- a/solution.py
+++ b/solution.py
@@ -67,7 +67,7 @@
     return depth * 3 // 4
 
 
-def turn(weight, step=512):
+def turn(weight, step=2048):
     depth, hidden_cols = weight.shape
     step = math.gcd(depth, step)
 
@@ -198,7 +198,7 @@
     block_rows = rows // wide
     share = half // narrow
     piece = math.gcd(block_rows, share)
-    tile = math.gcd(depth, 512)
+    tile = math.gcd(depth, 1024)
 
     def kernel(own_ref, other_ref, gate_ref, up_ref, *refs):
         out_refs, pre_ref = refs[:-1], refs[-1]

time: 50.4 us -> 50.4 us (level)
  no operation moved by 1% of the time
where the time goes in v5:
time: 50.4 us; the launch traced here: 50.2 us
  Pallas kernels  22 us (44%)
  starting transfers between devices  17.4 us (35%)
  waiting for transfers between devices  8.62 us (17%)
  other arithmetic  0.78 us (2%)
  between operations  0.76 us (2%)
  local copies, waits for them, and re-layouts  0.63 us (1%)
    ppermute x13, starting transfers between devices, exchange(): lax.ppermute(x, axis, [(i, partner(i, step, size)) for i in range(size)])  17.4 us
    ppermute x13, waiting for transfers between devices, exchange(): lax.ppermute(x, axis, [(i, partner(i, step, size)) for i in range(size)])  8.62 us
    pallas_call x1, Pallas kernels, load_turned(): pl.pallas_call(kernel, out_shape=[shape, pltpu.VMEM((hidden_cols, depth),...  7.95 us
    pallas_call x2, Pallas kernels, backward(): pl.pallas_call(kernel, out_shape=[jax.ShapeDtypeStruct((len(steps) * bloc...  5 us
    pallas_call x1, Pallas kernels, forward(): pl.pallas_call(kernel, out_shape=[jax.ShapeDtypeStruct(shape, jnp.float32...  4.95 us
    pallas_call x1, Pallas kernels, turn(): pl.pallas_call(kernel, out_shape=pltpu.VMEM((hidden_cols, depth), jnp.bfl...  3.92 us
  transfers between devices with their start and end apart: 13, of which 6 were waited for; matrix products, arithmetic and copies ran while one was open for 1% of the time, Pallas kernels for 29%

profile of v5, /device:TPU:0, one launch (start us, length us, event | category | flops | bytes accessed | tf_op | source)
XLA Modules:
  0.0 50.2 jit_solution(7236982668062956014)
XLA Ops:
  0.6 0.0 copy-start
  0.6 4.1 %collective-permute-start.1 = (bf16[16,4096]{1,0:T(8,128)(2,1)}, bf16[16,4096]{1,0:T(8,128)(2,1)S(1)}, u32[]{:S(2)}, u32[]{:S(2)}) collective-permute-start(bf16[16,4096]{1,0:T(8,128)(2,1)} %refs_0_), channel_id=1, source_target_pairs={{0,8},{4,12},{8,0},{12,4},{1,9},{5,13},{9,1},{13,5},{2,10},{6,14},... | collective-permute-start | bytes 393224 | tf_op jit(solution)/shard_map/ppermute | solution.py:25
  4.7 1.3 %collective-permute-start = (bf16[16,4096]{1,0:T(8,128)(2,1)}, bf16[16,4096]{1,0:T(8,128)(2,1)S(1)}, u32[]{:S(2)}, u32[]{:S(2)}) collective-permute-start(bf16[16,4096]{1,0:T(8,128)(2,1)} %refs_0_), channel_id=1, source_target_pairs={{0,12},{4,8},{8,4},{12,0},{1,13},{5,9},{9,5},{13,1},{2,14},{6,10},... | collective-permute-start | bytes 393224 | tf_op jit(solution)/shard_map/ppermute | solution.py:25
  6.1 0.2 collective-permute-start.2
  6.3 1.5 %collective-permute-start.3 = (bf16[16,1664]{1,0:T(8,128)(2,1)}, bf16[16,1664]{1,0:T(8,128)(2,1)S(1)}, u32[]{:S(2)}, u32[]{:S(2)}) collective-permute-start(bf16[16,1664]{1,0:T(8,128)(2,1)} %refs_2_), channel_id=1, source_target_pairs={{0,2},{2,0},{1,3},{3,1},{4,6},{6,4},{5,7},{7,5},{8,10},{10,8},{9,1... | collective-permute-start | bytes 159752 | tf_op jit(solution)/shard_map/ppermute | solution.py:25
  7.8 8.0 %load_turned.1 = (bf16[4096,1664]{1,0:T(8,128)(2,1)S(1)}, bf16[1664,4096]{1,0:T(8,128)(2,1)S(1)}, bf16[4096,1664]{1,0:T(8,128)(2,1)S(1)}) custom-call(bf16[4096,1664]{1,0:T(8,128)(2,1)} %hbm_ref.1, bf16[4096,1664]{1,0:T(8,128)(2,1)} %refs_5_.1), custom_call_target="tpu_custom_call" | custom-call | bytes 13631488 | tf_op jit(solution)/shard_map/load_turned/pallas_call | solution.py:54
  15.8 0.0 collective-permute-done.3.refs_3_
  15.8 0.0 collective-permute-done.1.refs_2_
  15.8 0.0 collective-permute-done.refs_1_
  15.8 0.0 collective-permute-done.2.refs_3_
  15.8 0.0 copy-done
  15.8 5.0 %forward.1 = (f32[32,3328]{1,0:T(8,128)S(1)}, bf16[32,3328]{1,0:T(8,128)(2,1)S(1)}, bf16[4096,1664]{1,0:T(8,128)(2,1)S(1)}) custom-call(bf16[16,4096]{1,0:T(8,128)(2,1)S(1)} %copy-done, bf16[16,4096]{1,0:T(8,128)(2,1)S(1)} %collective-permute-done.refs_1_, bf16[16,4096]{1,0:T(8,128)(2,1)S(1)} %collective-permute-done.1.refs_2_, ...), custom_call_target="tpu_custom_call", output_to_operand_aliasing={{2}: (6, {})} | custom-call | tf_op jit(solution)/shard_map/forward/pallas_call | solution.py:131
  20.8 0.1 collective-permute-start.4
  20.9 1.5 %collective-permute-done.4 = bf16[32,3328]{1,0:T(8,128)(2,1)S(1)} collective-permute-done((bf16[32,3328]{1,0:T(8,128)(2,1)S(1)}, bf16[32,3328]{1,0:T(8,128)(2,1)S(1)}, u32[]{:S(2)}, u32[]{:S(2)}) %collective-permute-start.4) | collective-permute-done | bytes 213024 | tf_op jit(solution)/shard_map/ppermute | solution.py:25
  22.4 0.0 copy-start.1
  22.4 1.2 %collective-permute-start.5 = (bf16[32,3328]{1,0:T(8,128)(2,1)S(1)}, bf16[32,3328]{1,0:T(8,128)(2,1)S(1)}, u32[]{:S(2)}, u32[]{:S(2)}) collective-permute-start(bf16[32,3328]{1,0:T(8,128)(2,1)S(1)} %get-tuple-element.38), channel_id=1, source_target_pairs={{0,2},{2,0},{1,3},{3,1},{4,6},{6,4},{5,7},{7,5},{8,10},{10,8},{9,1... | collective-permute-start | bytes 638984 | tf_op jit(solution)/shard_map/ppermute | solution.py:25
  23.6 3.9 %turn.1.up_ref = bf16[1664,4096]{1,0:T(8,128)(2,1)S(1)} custom-call(bf16[4096,1664]{1,0:T(8,128)(2,1)S(1)} %get-tuple-element.39.weight_ref), custom_call_target="tpu_custom_call" | custom-call | bytes 27262976 | tf_op jit(solution)/shard_map/turn/pallas_call | solution.py:82
  27.5 2.2 %collective-permute-done.5.refs_1_ = bf16[32,3328]{1,0:T(8,128)(2,1)S(1)} collective-permute-done((bf16[32,3328]{1,0:T(8,128)(2,1)S(1)}, bf16[32,3328]{1,0:T(8,128)(2,1)S(1)}, u32[]{:S(2)}, u32[]{:S(2)}) %collective-permute-start.5) | collective-permute-done | bytes 213024 | tf_op jit(solution)/shard_map/ppermute | solution.py:25
  29.7 0.0 copy-done.1
  29.7 0.2 activate.1
  29.9 0.1 collective-permute-start.6
  30.0 0.6 %copy.8 = bf16[16,1664]{1,0:T(8,128)(2,1)} copy(bf16[16,1664]{1,0:T(8,128)(2,1)S(1)} %get-tuple-element.56) | data formatting | bytes 106496
  30.6 0.8 %collective-permute-done.6.other_ref = bf16[32,3328]{1,0:T(8,128)(2,1)S(1)} collective-permute-done((bf16[32,3328]{1,0:T(8,128)(2,1)S(1)}, bf16[32,3328]{1,0:T(8,128)(2,1)S(1)}, u32[]{:S(2)}, u32[]{:S(2)}) %collective-permute-start.6) | collective-permute-done | bytes 213024 | tf_op jit(solution)/shard_map/ppermute | solution.py:25
  31.4 2.5 %backward.3 = (f32[16,2048]{1,0:T(8,128)S(1)}, bf16[16,2048]{1,0:T(8,128)(2,1)S(1)}, bf16[16,2048]{1,0:T(8,128)(2,1)S(1)}, bf16[16,2048]{1,0:T(8,128)(2,1)S(1)}) custom-call(bf16[32,3328]{1,0:T(8,128)(2,1)S(1)} %get-tuple-element.44.own_ref, bf16[32,3328]{1,0:T(8,128)(2,1)S(1)} %collective-permute-done.6.other_ref, ...), custom_call_target="tpu_custom_call" | custom-call | flops 872415232 | bytes 13631488 | tf_op jit(solution)/shard_map/backward/pallas_call | solution.py:221
  33.9 3.2 %collective-permute-start.10 = (bf16[16,2048]{1,0:T(8,128)(2,1)S(1)}, bf16[16,2048]{1,0:T(8,128)(2,1)S(1)}, u32[]{:S(2)}, u32[]{:S(2)}) collective-permute-start(bf16[16,2048]{1,0:T(8,128)(2,1)S(1)} %get-tuple-element.51), channel_id=1, source_target_pairs={{0,12},{4,8},{8,4},{12,0},{1,13},{5,9},{9,5},{13,1},{2,14},{6,10},... | collective-permute-start | bytes 196616 | tf_op jit(solution)/shard_map/ppermute | solution.py:25
  37.2 1.1 %collective-permute-start.11 = (bf16[16,2048]{1,0:T(8,128)(2,1)S(1)}, bf16[16,2048]{1,0:T(8,128)(2,1)S(1)}, u32[]{:S(2)}, u32[]{:S(2)}) collective-permute-start(bf16[16,2048]{1,0:T(8,128)(2,1)S(1)} %get-tuple-element.52), channel_id=1, source_target_pairs={{0,4},{4,0},{8,12},{12,8},{1,5},{5,1},{9,13},{13,9},{2,6},{6,2},{1... | collective-permute-start | bytes 196616 | tf_op jit(solution)/shard_map/ppermute | solution.py:25
  38.3 0.1 collective-permute-start.12
  38.4 2.5 %backward.2 = (f32[16,2048]{1,0:T(8,128)S(1)}, bf16[16,2048]{1,0:T(8,128)(2,1)S(1)}, bf16[16,2048]{1,0:T(8,128)(2,1)S(1)}, bf16[16,2048]{1,0:T(8,128)(2,1)S(1)}) custom-call(bf16[32,3328]{1,0:T(8,128)(2,1)S(1)} %get-tuple-element.44.own_ref, bf16[32,3328]{1,0:T(8,128)(2,1)S(1)} %collective-permute-done.6.other_ref, ...), custom_call_target="tpu_custom_call" | custom-call | flops 872415232 | bytes 13631488 | tf_op jit(solution)/shard_map/backward/pallas_call | solution.py:221
  40.9 3.2 %collective-permute-start.7 = (bf16[16,2048]{1,0:T(8,128)(2,1)S(1)}, bf16[16,2048]{1,0:T(8,128)(2,1)S(1)}, u32[]{:S(2)}, u32[]{:S(2)}) collective-permute-start(bf16[16,2048]{1,0:T(8,128)(2,1)S(1)} %get-tuple-element.47), channel_id=1, source_target_pairs={{0,12},{4,8},{8,4},{12,0},{1,13},{5,9},{9,5},{13,1},{2,14},{6,10},... | collective-permute-start | bytes 196616 | tf_op jit(solution)/shard_map/ppermute | solution.py:25
  44.1 0.2 collective-permute-start.8
  44.4 0.0 collective-permute-done.10
  44.4 1.0 %collective-permute-start.9 = (bf16[16,2048]{1,0:T(8,128)(2,1)S(1)}, bf16[16,2048]{1,0:T(8,128)(2,1)S(1)}, u32[]{:S(2)}, u32[]{:S(2)}) collective-permute-start(bf16[16,2048]{1,0:T(8,128)(2,1)S(1)} %get-tuple-element.49), channel_id=1, source_target_pairs={{0,8},{4,12},{8,0},{12,4},{1,9},{5,13},{9,1},{13,5},{2,10},{6,14},... | collective-permute-start | bytes 196616 | tf_op jit(solution)/shard_map/ppermute | solution.py:25
  45.4 0.0 collective-permute-done.11
  45.4 0.0 collective-permute-done.12
  45.4 1.8 %collective-permute-done.7 = bf16[16,2048]{1,0:T(8,128)(2,1)S(1)} collective-permute-done((bf16[16,2048]{1,0:T(8,128)(2,1)S(1)}, bf16[16,2048]{1,0:T(8,128)(2,1)S(1)}, u32[]{:S(2)}, u32[]{:S(2)}) %collective-permute-start.7) | collective-permute-done | bytes 65568 | tf_op jit(solution)/shard_map/ppermute | solution.py:25
  47.2 1.4 %collective-permute-done.8 = bf16[16,2048]{1,0:T(8,128)(2,1)S(1)} collective-permute-done((bf16[16,2048]{1,0:T(8,128)(2,1)S(1)}, bf16[16,2048]{1,0:T(8,128)(2,1)S(1)}, u32[]{:S(2)}, u32[]{:S(2)}) %collective-permute-start.8) | collective-permute-done | bytes 65568 | tf_op jit(solution)/shard_map/ppermute | solution.py:25
  48.5 1.0 %collective-permute-done.9 = bf16[16,2048]{1,0:T(8,128)(2,1)S(1)} collective-permute-done((bf16[16,2048]{1,0:T(8,128)(2,1)S(1)}, bf16[16,2048]{1,0:T(8,128)(2,1)S(1)}, u32[]{:S(2)}, u32[]{:S(2)}) %collective-permute-start.9) | collective-permute-done | bytes 65568 | tf_op jit(solution)/shard_map/ppermute | solution.py:25
  49.6 0.7 %pad_maximum_fusion = bf16[16,4096]{1,0:T(8,128)(2,1)} fusion(bf16[16,2048]{1,0:T(8,128)(2,1)S(1)} %add_convert_fusion, bf16[16,2048]{1,0:T(8,128)(2,1)S(1)} %add_convert_fusion.1), kind=kLoop, calls=%fused_computation.1 | loop fusion | flops 262144 | bytes 262144 | tf_op jit(solution)/shard_map/concatenate | solution.py:268
  (3 shorter events, 0.1 us)
Async XLA Ops:
  0.6 15.2 %copy-start = (bf16[16,4096]{1,0:T(8,128)(2,1)S(1)}, bf16[16,4096]{1,0:T(8,128)(2,1)}, u32[]{:S(2)}) copy-start(bf16[16,4096]{1,0:T(8,128)(2,1)} %refs_0_) | copy-start | bytes 393220
  0.6 15.1 %collective-permute-start.1 = (bf16[16,4096]{1,0:T(8,128)(2,1)}, bf16[16,4096]{1,0:T(8,128)(2,1)S(1)}, u32[]{:S(2)}, u32[]{:S(2)}) collective-permute-start(bf16[16,4096]{1,0:T(8,128)(2,1)} %refs_0_), channel_id=1, source_target_pairs={{0,8},{4,12},{8,0},{12,4},{1,9},{5,13},{9,1},{13,5},{2,10},{6,14},... | collective-permute-start | bytes 393224 | tf_op jit(solution)/shard_map/ppermute | solution.py:25
  4.7 11.1 %collective-permute-start = (bf16[16,4096]{1,0:T(8,128)(2,1)}, bf16[16,4096]{1,0:T(8,128)(2,1)S(1)}, u32[]{:S(2)}, u32[]{:S(2)}) collective-permute-start(bf16[16,4096]{1,0:T(8,128)(2,1)} %refs_0_), channel_id=1, source_target_pairs={{0,12},{4,8},{8,4},{12,0},{1,13},{5,9},{9,5},{13,1},{2,14},{6,10},... | collective-permute-start | bytes 393224 | tf_op jit(solution)/shard_map/ppermute | solution.py:25
  6.1 9.7 %collective-permute-start.2 = (bf16[16,4096]{1,0:T(8,128)(2,1)}, bf16[16,4096]{1,0:T(8,128)(2,1)S(1)}, u32[]{:S(2)}, u32[]{:S(2)}) collective-permute-start(bf16[16,4096]{1,0:T(8,128)(2,1)} %refs_0_), channel_id=1, source_target_pairs={{0,4},{4,0},{8,12},{12,8},{1,5},{5,1},{9,13},{13,9},{2,6},{6,2},{1... | collective-permute-start | bytes 393224 | tf_op jit(solution)/shard_map/ppermute | solution.py:25
  6.3 9.5 %collective-permute-start.3 = (bf16[16,1664]{1,0:T(8,128)(2,1)}, bf16[16,1664]{1,0:T(8,128)(2,1)S(1)}, u32[]{:S(2)}, u32[]{:S(2)}) collective-permute-start(bf16[16,1664]{1,0:T(8,128)(2,1)} %refs_2_), channel_id=1, source_target_pairs={{0,2},{2,0},{1,3},{3,1},{4,6},{6,4},{5,7},{7,5},{8,10},{10,8},{9,1... | collective-permute-start | bytes 159752 | tf_op jit(solution)/shard_map/ppermute | solution.py:25
  20.8 1.5 %collective-permute-start.4 = (bf16[32,3328]{1,0:T(8,128)(2,1)S(1)}, bf16[32,3328]{1,0:T(8,128)(2,1)S(1)}, u32[]{:S(2)}, u32[]{:S(2)}) collective-permute-start(bf16[32,3328]{1,0:T(8,128)(2,1)S(1)} %get-tuple-element.36), channel_id=1, source_target_pairs={{0,1},{1,0},{2,3},{3,2},{4,5},{5,4},{6,7},{7,6},{8,9},{9,8},{10,11... | collective-permute-start | bytes 638984 | tf_op jit(solution)/shard_map/ppermute | solution.py:25
  22.4 7.4 %copy-start.1 = (bf16[16,1664]{1,0:T(8,128)(2,1)S(1)}, bf16[16,1664]{1,0:T(8,128)(2,1)}, u32[]{:S(2)}) copy-start(bf16[16,1664]{1,0:T(8,128)(2,1)} %refs_2_) | copy-start | bytes 159748
  22.4 7.4 %collective-permute-start.5 = (bf16[32,3328]{1,0:T(8,128)(2,1)S(1)}, bf16[32,3328]{1,0:T(8,128)(2,1)S(1)}, u32[]{:S(2)}, u32[]{:S(2)}) collective-permute-start(bf16[32,3328]{1,0:T(8,128)(2,1)S(1)} %get-tuple-element.38), channel_id=1, source_target_pairs={{0,2},{2,0},{1,3},{3,1},{4,6},{6,4},{5,7},{7,5},{8,10},{10,8},{9,1... | collective-permute-start | bytes 638984 | tf_op jit(solution)/shard_map/ppermute | solution.py:25
  29.9 1.5 %collective-permute-start.6 = (bf16[32,3328]{1,0:T(8,128)(2,1)S(1)}, bf16[32,3328]{1,0:T(8,128)(2,1)S(1)}, u32[]{:S(2)}, u32[]{:S(2)}) collective-permute-start(bf16[32,3328]{1,0:T(8,128)(2,1)S(1)} %get-tuple-element.44.own_ref), channel_id=1, source_target_pairs={{0,1},{1,0},{2,3},{3,2},{4,5},{5,4},{6,7},{7,6},{8,9},{9,8},{10,11... | collective-permute-start | bytes 638984 | tf_op jit(solution)/shard_map/ppermute | solution.py:25
  33.9 10.4 %collective-permute-start.10 = (bf16[16,2048]{1,0:T(8,128)(2,1)S(1)}, bf16[16,2048]{1,0:T(8,128)(2,1)S(1)}, u32[]{:S(2)}, u32[]{:S(2)}) collective-permute-start(bf16[16,2048]{1,0:T(8,128)(2,1)S(1)} %get-tuple-element.51), channel_id=1, source_target_pairs={{0,12},{4,8},{8,4},{12,0},{1,13},{5,9},{9,5},{13,1},{2,14},{6,10},... | collective-permute-start | bytes 196616 | tf_op jit(solution)/shard_map/ppermute | solution.py:25
  37.2 8.2 %collective-permute-start.11 = (bf16[16,2048]{1,0:T(8,128)(2,1)S(1)}, bf16[16,2048]{1,0:T(8,128)(2,1)S(1)}, u32[]{:S(2)}, u32[]{:S(2)}) collective-permute-start(bf16[16,2048]{1,0:T(8,128)(2,1)S(1)} %get-tuple-element.52), channel_id=1, source_target_pairs={{0,4},{4,0},{8,12},{12,8},{1,5},{5,1},{9,13},{13,9},{2,6},{6,2},{1... | collective-permute-start | bytes 196616 | tf_op jit(solution)/shard_map/ppermute | solution.py:25
  38.3 7.1 %collective-permute-start.12 = (bf16[16,2048]{1,0:T(8,128)(2,1)S(1)}, bf16[16,2048]{1,0:T(8,128)(2,1)S(1)}, u32[]{:S(2)}, u32[]{:S(2)}) collective-permute-start(bf16[16,2048]{1,0:T(8,128)(2,1)S(1)} %get-tuple-element.53), channel_id=1, source_target_pairs={{0,8},{4,12},{8,0},{12,4},{1,9},{5,13},{9,1},{13,5},{2,10},{6,14},... | collective-permute-start | bytes 196616 | tf_op jit(solution)/shard_map/ppermute | solution.py:25
  40.9 6.3 %collective-permute-start.7 = (bf16[16,2048]{1,0:T(8,128)(2,1)S(1)}, bf16[16,2048]{1,0:T(8,128)(2,1)S(1)}, u32[]{:S(2)}, u32[]{:S(2)}) collective-permute-start(bf16[16,2048]{1,0:T(8,128)(2,1)S(1)} %get-tuple-element.47), channel_id=1, source_target_pairs={{0,12},{4,8},{8,4},{12,0},{1,13},{5,9},{9,5},{13,1},{2,14},{6,10},... | collective-permute-start | bytes 196616 | tf_op jit(solution)/shard_map/ppermute | solution.py:25
  44.1 4.4 %collective-permute-start.8 = (bf16[16,2048]{1,0:T(8,128)(2,1)S(1)}, bf16[16,2048]{1,0:T(8,128)(2,1)S(1)}, u32[]{:S(2)}, u32[]{:S(2)}) collective-permute-start(bf16[16,2048]{1,0:T(8,128)(2,1)S(1)} %get-tuple-element.48), channel_id=1, source_target_pairs={{0,4},{4,0},{8,12},{12,8},{1,5},{5,1},{9,13},{13,9},{2,6},{6,2},{1... | collective-permute-start | bytes 196616 | tf_op jit(solution)/shard_map/ppermute | solution.py:25
  44.4 5.2 %collective-permute-start.9 = (bf16[16,2048]{1,0:T(8,128)(2,1)S(1)}, bf16[16,2048]{1,0:T(8,128)(2,1)S(1)}, u32[]{:S(2)}, u32[]{:S(2)}) collective-permute-start(bf16[16,2048]{1,0:T(8,128)(2,1)S(1)} %get-tuple-element.49), channel_id=1, source_target_pairs={{0,8},{4,12},{8,0},{12,4},{1,9},{5,13},{9,1},{13,5},{2,10},{6,14},... | collective-permute-start | bytes 196616 | tf_op jit(solution)/shard_map/ppermute | solution.py:25

commit v6 on v5

--- a/solution.py
+++ b/solution.py
@@ -64,7 +64,7 @@
 
 
 def ahead_rows(depth):
-    return depth * 3 // 4
+    return depth * 5 // 8
 
 
 def turn(weight, step=2048):
@@ -234,7 +234,7 @@
 
 def shards(tokens, gate_weight, up_weight, hidden_grad, sizes):
     wide, narrow, sub = sizes
-    order = [3, 2, 1] if wide == 4 else list(range(1, wide))
+    order = [2, 3, 1] if wide == 4 else list(range(1, wide))
     got = {step: exchange(tokens, "wide", step, wide) for step in order}
     steps = [0] + order
     blocks = [tokens] + [got[step] for step in order]
@@ -262,7 +262,7 @@
     for part in range(PARTS):
         own, *sends = bwd(begin=part * width, depth=width, groups=direct)
         sends = dict(zip(order, sends))
-        turns = [3, 1, 2] if wide == 4 else order
+        turns = ([3, 1, 2], [2, 3, 1])[part] if wide == 4 else order
         got = [exchange(sends[step], "wide", step, wide) for step in turns]
         totals.append(own + sum(x.astype(f32) for x in got))
     return (hidden, jnp.concatenate([total.astype(bf16) for total in totals], axis=1))

time: 50.4 us -> 50.2 us (level)
  waiting for transfers between devices: 8.62 us -> 9.23 us
    ppermute x13, waiting for transfers between devices: 8.62 us -> 9.23 us  [exchange(): lax.ppermute(x, axis, [(i, partner(i, step, size)) for i in range(size)])]
  transfers between devices with their start and end apart: 13 -> 13, of which waited for: 6 -> 7; matrix products, arithmetic and copies ran while one was open for 1% -> 1% of each run, Pallas kernels for 29% -> 28%
where the time goes in v6:
time: 50.2 us; the launch traced here: 50 us
  Pallas kernels  21.5 us (43%)
  starting transfers between devices  17.1 us (34%)
  waiting for transfers between devices  9.23 us (18%)
  other arithmetic  0.78 us (2%)
  between operations  0.74 us (1%)
  local copies, waits for them, and re-layouts  0.63 us (1%)
    ppermute x13, starting transfers between devices, exchange(): lax.ppermute(x, axis, [(i, partner(i, step, size)) for i in range(size)])  17.1 us
    ppermute x13, waiting for transfers between devices, exchange(): lax.ppermute(x, axis, [(i, partner(i, step, size)) for i in range(size)])  9.23 us
    pallas_call x1, Pallas kernels, load_turned(): pl.pallas_call(kernel, out_shape=[shape, pltpu.VMEM((hidden_cols, depth),...  7.47 us
    pallas_call x2, Pallas kernels, backward(): pl.pallas_call(kernel, out_shape=[jax.ShapeDtypeStruct((len(steps) * bloc...  5.01 us
    pallas_call x1, Pallas kernels, forward(): pl.pallas_call(kernel, out_shape=[jax.ShapeDtypeStruct(shape, jnp.float32...  4.96 us
    pallas_call x1, Pallas kernels, turn(): pl.pallas_call(kernel, out_shape=pltpu.VMEM((hidden_cols, depth), jnp.bfl...  3.92 us
  transfers between devices with their start and end apart: 13, of which 7 were waited for; matrix products, arithmetic and copies ran while one was open for 1% of the time, Pallas kernels for 28%

profile of v6, /device:TPU:0, one launch (start us, length us, event | category | flops | bytes accessed | tf_op | source)
XLA Modules:
  0.0 50.0 jit_solution(9272174779413151384)
XLA Ops:
  0.6 0.0 copy-start
  0.6 5.1 %collective-permute-start.1 = (bf16[16,4096]{1,0:T(8,128)(2,1)}, bf16[16,4096]{1,0:T(8,128)(2,1)S(1)}, u32[]{:S(2)}, u32[]{:S(2)}) collective-permute-start(bf16[16,4096]{1,0:T(8,128)(2,1)} %refs_0_), channel_id=1, source_target_pairs={{0,12},{4,8},{8,4},{12,0},{1,13},{5,9},{9,5},{13,1},{2,14},{6,10},... | collective-permute-start | bytes 393224 | tf_op jit(solution)/shard_map/ppermute | solution.py:25
  5.8 0.0 collective-permute-start
  5.8 0.6 %collective-permute-start.2 = (bf16[16,4096]{1,0:T(8,128)(2,1)}, bf16[16,4096]{1,0:T(8,128)(2,1)S(1)}, u32[]{:S(2)}, u32[]{:S(2)}) collective-permute-start(bf16[16,4096]{1,0:T(8,128)(2,1)} %refs_0_), channel_id=1, source_target_pairs={{0,4},{4,0},{8,12},{12,8},{1,5},{5,1},{9,13},{13,9},{2,6},{6,2},{1... | collective-permute-start | bytes 393224 | tf_op jit(solution)/shard_map/ppermute | solution.py:25
  6.4 1.6 %collective-permute-start.3 = (bf16[16,1664]{1,0:T(8,128)(2,1)}, bf16[16,1664]{1,0:T(8,128)(2,1)S(1)}, u32[]{:S(2)}, u32[]{:S(2)}) collective-permute-start(bf16[16,1664]{1,0:T(8,128)(2,1)} %refs_2_), channel_id=1, source_target_pairs={{0,2},{2,0},{1,3},{3,1},{4,6},{6,4},{5,7},{7,5},{8,10},{10,8},{9,1... | collective-permute-start | bytes 159752 | tf_op jit(solution)/shard_map/ppermute | solution.py:25
  8.0 7.5 %load_turned.1 = (bf16[4096,1664]{1,0:T(8,128)(2,1)S(1)}, bf16[1664,4096]{1,0:T(8,128)(2,1)S(1)}, bf16[4096,1664]{1,0:T(8,128)(2,1)S(1)}) custom-call(bf16[4096,1664]{1,0:T(8,128)(2,1)} %hbm_ref.1, bf16[4096,1664]{1,0:T(8,128)(2,1)} %refs_5_.1), custom_call_target="tpu_custom_call" | custom-call | bytes 13631488 | tf_op jit(solution)/shard_map/load_turned/pallas_call | solution.py:54
  15.5 0.0 collective-permute-done.3.refs_3_
  15.5 0.0 collective-permute-done.1.refs_2_
  15.5 1.5 %collective-permute-done.refs_1_ = bf16[16,4096]{1,0:T(8,128)(2,1)S(1)} collective-permute-done((bf16[16,4096]{1,0:T(8,128)(2,1)}, bf16[16,4096]{1,0:T(8,128)(2,1)S(1)}, u32[]{:S(2)}, u32[]{:S(2)}) %collective-permute-start) | collective-permute-done | bytes 131104 | tf_op jit(solution)/shard_map/ppermute | solution.py:25
  17.0 0.0 collective-permute-done.2.refs_3_
  17.0 0.0 copy-done
  17.0 5.0 %forward.1 = (f32[32,3328]{1,0:T(8,128)S(1)}, bf16[32,3328]{1,0:T(8,128)(2,1)S(1)}, bf16[4096,1664]{1,0:T(8,128)(2,1)S(1)}) custom-call(bf16[16,4096]{1,0:T(8,128)(2,1)S(1)} %copy-done, bf16[16,4096]{1,0:T(8,128)(2,1)S(1)} %collective-permute-done.refs_1_, bf16[16,4096]{1,0:T(8,128)(2,1)S(1)} %collective-permute-done.1.refs_2_, ...), custom_call_target="tpu_custom_call", output_to_operand_aliasing={{2}: (6, {})} | custom-call | tf_op jit(solution)/shard_map/forward/pallas_call | solution.py:131
  22.0 0.1 collective-permute-start.4
  22.1 1.5 %collective-permute-done.4 = bf16[32,3328]{1,0:T(8,128)(2,1)S(1)} collective-permute-done((bf16[32,3328]{1,0:T(8,128)(2,1)S(1)}, bf16[32,3328]{1,0:T(8,128)(2,1)S(1)}, u32[]{:S(2)}, u32[]{:S(2)}) %collective-permute-start.4) | collective-permute-done | bytes 213024 | tf_op jit(solution)/shard_map/ppermute | solution.py:25
  23.6 0.0 copy-start.1
  23.6 1.6 %collective-permute-start.5 = (bf16[32,3328]{1,0:T(8,128)(2,1)S(1)}, bf16[32,3328]{1,0:T(8,128)(2,1)S(1)}, u32[]{:S(2)}, u32[]{:S(2)}) collective-permute-start(bf16[32,3328]{1,0:T(8,128)(2,1)S(1)} %get-tuple-element.38), channel_id=1, source_target_pairs={{0,2},{2,0},{1,3},{3,1},{4,6},{6,4},{5,7},{7,5},{8,10},{10,8},{9,1... | collective-permute-start | bytes 638984 | tf_op jit(solution)/shard_map/ppermute | solution.py:25
  25.2 3.9 %turn.1.up_ref = bf16[1664,4096]{1,0:T(8,128)(2,1)S(1)} custom-call(bf16[4096,1664]{1,0:T(8,128)(2,1)S(1)} %get-tuple-element.39.weight_ref), custom_call_target="tpu_custom_call" | custom-call | bytes 27262976 | tf_op jit(solution)/shard_map/turn/pallas_call | solution.py:82
  29.1 1.9 %collective-permute-done.5.refs_1_ = bf16[32,3328]{1,0:T(8,128)(2,1)S(1)} collective-permute-done((bf16[32,3328]{1,0:T(8,128)(2,1)S(1)}, bf16[32,3328]{1,0:T(8,128)(2,1)S(1)}, u32[]{:S(2)}, u32[]{:S(2)}) %collective-permute-start.5) | collective-permute-done | bytes 213024 | tf_op jit(solution)/shard_map/ppermute | solution.py:25
  31.0 0.0 copy-done.1
  31.0 0.2 activate.1
  31.1 0.1 collective-permute-start.6
  31.2 0.6 %copy.8 = bf16[16,1664]{1,0:T(8,128)(2,1)} copy(bf16[16,1664]{1,0:T(8,128)(2,1)S(1)} %get-tuple-element.56) | data formatting | bytes 106496
  31.8 0.8 %collective-permute-done.6.other_ref = bf16[32,3328]{1,0:T(8,128)(2,1)S(1)} collective-permute-done((bf16[32,3328]{1,0:T(8,128)(2,1)S(1)}, bf16[32,3328]{1,0:T(8,128)(2,1)S(1)}, u32[]{:S(2)}, u32[]{:S(2)}) %collective-permute-start.6) | collective-permute-done | bytes 213024 | tf_op jit(solution)/shard_map/ppermute | solution.py:25
  32.7 2.5 %backward.3 = (f32[16,2048]{1,0:T(8,128)S(1)}, bf16[16,2048]{1,0:T(8,128)(2,1)S(1)}, bf16[16,2048]{1,0:T(8,128)(2,1)S(1)}, bf16[16,2048]{1,0:T(8,128)(2,1)S(1)}) custom-call(bf16[32,3328]{1,0:T(8,128)(2,1)S(1)} %get-tuple-element.44.own_ref, bf16[32,3328]{1,0:T(8,128)(2,1)S(1)} %collective-permute-done.6.other_ref, ...), custom_call_target="tpu_custom_call" | custom-call | flops 872415232 | bytes 13631488 | tf_op jit(solution)/shard_map/backward/pallas_call | solution.py:221
  35.2 0.7 %collective-permute-start.10 = (bf16[16,2048]{1,0:T(8,128)(2,1)S(1)}, bf16[16,2048]{1,0:T(8,128)(2,1)S(1)}, u32[]{:S(2)}, u32[]{:S(2)}) collective-permute-start(bf16[16,2048]{1,0:T(8,128)(2,1)S(1)} %get-tuple-element.51), channel_id=1, source_target_pairs={{0,8},{4,12},{8,0},{12,4},{1,9},{5,13},{9,1},{13,5},{2,10},{6,14},... | collective-permute-start | bytes 196616 | tf_op jit(solution)/shard_map/ppermute | solution.py:25
  35.9 1.9 %collective-permute-start.11 = (bf16[16,2048]{1,0:T(8,128)(2,1)S(1)}, bf16[16,2048]{1,0:T(8,128)(2,1)S(1)}, u32[]{:S(2)}, u32[]{:S(2)}) collective-permute-start(bf16[16,2048]{1,0:T(8,128)(2,1)S(1)} %get-tuple-element.52), channel_id=1, source_target_pairs={{0,12},{4,8},{8,4},{12,0},{1,13},{5,9},{9,5},{13,1},{2,14},{6,10},... | collective-permute-start | bytes 196616 | tf_op jit(solution)/shard_map/ppermute | solution.py:25
  37.8 0.9 %collective-permute-start.12 = (bf16[16,2048]{1,0:T(8,128)(2,1)S(1)}, bf16[16,2048]{1,0:T(8,128)(2,1)S(1)}, u32[]{:S(2)}, u32[]{:S(2)}) collective-permute-start(bf16[16,2048]{1,0:T(8,128)(2,1)S(1)} %get-tuple-element.53), channel_id=1, source_target_pairs={{0,4},{4,0},{8,12},{12,8},{1,5},{5,1},{9,13},{13,9},{2,6},{6,2},{1... | collective-permute-start | bytes 196616 | tf_op jit(solution)/shard_map/ppermute | solution.py:25
  38.7 2.5 %backward.2 = (f32[16,2048]{1,0:T(8,128)S(1)}, bf16[16,2048]{1,0:T(8,128)(2,1)S(1)}, bf16[16,2048]{1,0:T(8,128)(2,1)S(1)}, bf16[16,2048]{1,0:T(8,128)(2,1)S(1)}) custom-call(bf16[32,3328]{1,0:T(8,128)(2,1)S(1)} %get-tuple-element.44.own_ref, bf16[32,3328]{1,0:T(8,128)(2,1)S(1)} %collective-permute-done.6.other_ref, ...), custom_call_target="tpu_custom_call" | custom-call | flops 872415232 | bytes 13631488 | tf_op jit(solution)/shard_map/backward/pallas_call | solution.py:221
  41.2 2.6 %collective-permute-start.7 = (bf16[16,2048]{1,0:T(8,128)(2,1)S(1)}, bf16[16,2048]{1,0:T(8,128)(2,1)S(1)}, u32[]{:S(2)}, u32[]{:S(2)}) collective-permute-start(bf16[16,2048]{1,0:T(8,128)(2,1)S(1)} %get-tuple-element.47), channel_id=1, source_target_pairs={{0,12},{4,8},{8,4},{12,0},{1,13},{5,9},{9,5},{13,1},{2,14},{6,10},... | collective-permute-start | bytes 196616 | tf_op jit(solution)/shard_map/ppermute | solution.py:25
  43.8 0.0 collective-permute-start.8
  43.8 0.0 collective-permute-done.10
  43.8 1.9 %collective-permute-start.9 = (bf16[16,2048]{1,0:T(8,128)(2,1)S(1)}, bf16[16,2048]{1,0:T(8,128)(2,1)S(1)}, u32[]{:S(2)}, u32[]{:S(2)}) collective-permute-start(bf16[16,2048]{1,0:T(8,128)(2,1)S(1)} %get-tuple-element.49), channel_id=1, source_target_pairs={{0,8},{4,12},{8,0},{12,4},{1,9},{5,13},{9,1},{13,5},{2,10},{6,14},... | collective-permute-start | bytes 196616 | tf_op jit(solution)/shard_map/ppermute | solution.py:25
  45.7 0.0 collective-permute-done.11
  45.7 0.0 collective-permute-done.12
  45.7 1.7 %collective-permute-done.7 = bf16[16,2048]{1,0:T(8,128)(2,1)S(1)} collective-permute-done((bf16[16,2048]{1,0:T(8,128)(2,1)S(1)}, bf16[16,2048]{1,0:T(8,128)(2,1)S(1)}, u32[]{:S(2)}, u32[]{:S(2)}) %collective-permute-start.7) | collective-permute-done | bytes 65568 | tf_op jit(solution)/shard_map/ppermute | solution.py:25
  47.5 1.3 %collective-permute-done.8 = bf16[16,2048]{1,0:T(8,128)(2,1)S(1)} collective-permute-done((bf16[16,2048]{1,0:T(8,128)(2,1)S(1)}, bf16[16,2048]{1,0:T(8,128)(2,1)S(1)}, u32[]{:S(2)}, u32[]{:S(2)}) %collective-permute-start.8) | collective-permute-done | bytes 65568 | tf_op jit(solution)/shard_map/ppermute | solution.py:25
  48.8 0.5 %collective-permute-done.9 = bf16[16,2048]{1,0:T(8,128)(2,1)S(1)} collective-permute-done((bf16[16,2048]{1,0:T(8,128)(2,1)S(1)}, bf16[16,2048]{1,0:T(8,128)(2,1)S(1)}, u32[]{:S(2)}, u32[]{:S(2)}) %collective-permute-start.9) | collective-permute-done | bytes 65568 | tf_op jit(solution)/shard_map/ppermute | solution.py:25
  49.3 0.7 %pad_maximum_fusion = bf16[16,4096]{1,0:T(8,128)(2,1)} fusion(bf16[16,2048]{1,0:T(8,128)(2,1)S(1)} %add_convert_fusion, bf16[16,2048]{1,0:T(8,128)(2,1)S(1)} %add_convert_fusion.1), kind=kLoop, calls=%fused_computation.1 | loop fusion | flops 262144 | bytes 262144 | tf_op jit(solution)/shard_map/concatenate | solution.py:268
  (3 shorter events, 0.1 us)
Async XLA Ops:
  0.6 16.4 %copy-start = (bf16[16,4096]{1,0:T(8,128)(2,1)S(1)}, bf16[16,4096]{1,0:T(8,128)(2,1)}, u32[]{:S(2)}) copy-start(bf16[16,4096]{1,0:T(8,128)(2,1)} %refs_0_) | copy-start | bytes 393220
  0.6 14.9 %collective-permute-start.1 = (bf16[16,4096]{1,0:T(8,128)(2,1)}, bf16[16,4096]{1,0:T(8,128)(2,1)S(1)}, u32[]{:S(2)}, u32[]{:S(2)}) collective-permute-start(bf16[16,4096]{1,0:T(8,128)(2,1)} %refs_0_), channel_id=1, source_target_pairs={{0,12},{4,8},{8,4},{12,0},{1,13},{5,9},{9,5},{13,1},{2,14},{6,10},... | collective-permute-start | bytes 393224 | tf_op jit(solution)/shard_map/ppermute | solution.py:25
  5.8 11.3 %collective-permute-start = (bf16[16,4096]{1,0:T(8,128)(2,1)}, bf16[16,4096]{1,0:T(8,128)(2,1)S(1)}, u32[]{:S(2)}, u32[]{:S(2)}) collective-permute-start(bf16[16,4096]{1,0:T(8,128)(2,1)} %refs_0_), channel_id=1, source_target_pairs={{0,8},{4,12},{8,0},{12,4},{1,9},{5,13},{9,1},{13,5},{2,10},{6,14},... | collective-permute-start | bytes 393224 | tf_op jit(solution)/shard_map/ppermute | solution.py:25
  5.8 11.3 %collective-permute-start.2 = (bf16[16,4096]{1,0:T(8,128)(2,1)}, bf16[16,4096]{1,0:T(8,128)(2,1)S(1)}, u32[]{:S(2)}, u32[]{:S(2)}) collective-permute-start(bf16[16,4096]{1,0:T(8,128)(2,1)} %refs_0_), channel_id=1, source_target_pairs={{0,4},{4,0},{8,12},{12,8},{1,5},{5,1},{9,13},{13,9},{2,6},{6,2},{1... | collective-permute-start | bytes 393224 | tf_op jit(solution)/shard_map/ppermute | solution.py:25
  6.4 9.1 %collective-permute-start.3 = (bf16[16,1664]{1,0:T(8,128)(2,1)}, bf16[16,1664]{1,0:T(8,128)(2,1)S(1)}, u32[]{:S(2)}, u32[]{:S(2)}) collective-permute-start(bf16[16,1664]{1,0:T(8,128)(2,1)} %refs_2_), channel_id=1, source_target_pairs={{0,2},{2,0},{1,3},{3,1},{4,6},{6,4},{5,7},{7,5},{8,10},{10,8},{9,1... | collective-permute-start | bytes 159752 | tf_op jit(solution)/shard_map/ppermute | solution.py:25
  22.0 1.5 %collective-permute-start.4 = (bf16[32,3328]{1,0:T(8,128)(2,1)S(1)}, bf16[32,3328]{1,0:T(8,128)(2,1)S(1)}, u32[]{:S(2)}, u32[]{:S(2)}) collective-permute-start(bf16[32,3328]{1,0:T(8,128)(2,1)S(1)} %get-tuple-element.36), channel_id=1, source_target_pairs={{0,1},{1,0},{2,3},{3,2},{4,5},{5,4},{6,7},{7,6},{8,9},{9,8},{10,11... | collective-permute-start | bytes 638984 | tf_op jit(solution)/shard_map/ppermute | solution.py:25
  23.6 7.4 %copy-start.1 = (bf16[16,1664]{1,0:T(8,128)(2,1)S(1)}, bf16[16,1664]{1,0:T(8,128)(2,1)}, u32[]{:S(2)}) copy-start(bf16[16,1664]{1,0:T(8,128)(2,1)} %refs_2_) | copy-start | bytes 159748
  23.6 7.4 %collective-permute-start.5 = (bf16[32,3328]{1,0:T(8,128)(2,1)S(1)}, bf16[32,3328]{1,0:T(8,128)(2,1)S(1)}, u32[]{:S(2)}, u32[]{:S(2)}) collective-permute-start(bf16[32,3328]{1,0:T(8,128)(2,1)S(1)} %get-tuple-element.38), channel_id=1, source_target_pairs={{0,2},{2,0},{1,3},{3,1},{4,6},{6,4},{5,7},{7,5},{8,10},{10,8},{9,1... | collective-permute-start | bytes 638984 | tf_op jit(solution)/shard_map/ppermute | solution.py:25
  31.1 1.5 %collective-permute-start.6 = (bf16[32,3328]{1,0:T(8,128)(2,1)S(1)}, bf16[32,3328]{1,0:T(8,128)(2,1)S(1)}, u32[]{:S(2)}, u32[]{:S(2)}) collective-permute-start(bf16[32,3328]{1,0:T(8,128)(2,1)S(1)} %get-tuple-element.44.own_ref), channel_id=1, source_target_pairs={{0,1},{1,0},{2,3},{3,2},{4,5},{5,4},{6,7},{7,6},{8,9},{9,8},{10,11... | collective-permute-start | bytes 638984 | tf_op jit(solution)/shard_map/ppermute | solution.py:25
  35.2 8.6 %collective-permute-start.10 = (bf16[16,2048]{1,0:T(8,128)(2,1)S(1)}, bf16[16,2048]{1,0:T(8,128)(2,1)S(1)}, u32[]{:S(2)}, u32[]{:S(2)}) collective-permute-start(bf16[16,2048]{1,0:T(8,128)(2,1)S(1)} %get-tuple-element.51), channel_id=1, source_target_pairs={{0,8},{4,12},{8,0},{12,4},{1,9},{5,13},{9,1},{13,5},{2,10},{6,14},... | collective-permute-start | bytes 196616 | tf_op jit(solution)/shard_map/ppermute | solution.py:25
  35.9 9.8 %collective-permute-start.11 = (bf16[16,2048]{1,0:T(8,128)(2,1)S(1)}, bf16[16,2048]{1,0:T(8,128)(2,1)S(1)}, u32[]{:S(2)}, u32[]{:S(2)}) collective-permute-start(bf16[16,2048]{1,0:T(8,128)(2,1)S(1)} %get-tuple-element.52), channel_id=1, source_target_pairs={{0,12},{4,8},{8,4},{12,0},{1,13},{5,9},{9,5},{13,1},{2,14},{6,10},... | collective-permute-start | bytes 196616 | tf_op jit(solution)/shard_map/ppermute | solution.py:25
  37.8 7.9 %collective-permute-start.12 = (bf16[16,2048]{1,0:T(8,128)(2,1)S(1)}, bf16[16,2048]{1,0:T(8,128)(2,1)S(1)}, u32[]{:S(2)}, u32[]{:S(2)}) collective-permute-start(bf16[16,2048]{1,0:T(8,128)(2,1)S(1)} %get-tuple-element.53), channel_id=1, source_target_pairs={{0,4},{4,0},{8,12},{12,8},{1,5},{5,1},{9,13},{13,9},{2,6},{6,2},{1... | collective-permute-start | bytes 196616 | tf_op jit(solution)/shard_map/ppermute | solution.py:25
  41.2 6.2 %collective-permute-start.7 = (bf16[16,2048]{1,0:T(8,128)(2,1)S(1)}, bf16[16,2048]{1,0:T(8,128)(2,1)S(1)}, u32[]{:S(2)}, u32[]{:S(2)}) collective-permute-start(bf16[16,2048]{1,0:T(8,128)(2,1)S(1)} %get-tuple-element.47), channel_id=1, source_target_pairs={{0,12},{4,8},{8,4},{12,0},{1,13},{5,9},{9,5},{13,1},{2,14},{6,10},... | collective-permute-start | bytes 196616 | tf_op jit(solution)/shard_map/ppermute | solution.py:25
  43.8 5.0 %collective-permute-start.8 = (bf16[16,2048]{1,0:T(8,128)(2,1)S(1)}, bf16[16,2048]{1,0:T(8,128)(2,1)S(1)}, u32[]{:S(2)}, u32[]{:S(2)}) collective-permute-start(bf16[16,2048]{1,0:T(8,128)(2,1)S(1)} %get-tuple-element.48), channel_id=1, source_target_pairs={{0,4},{4,0},{8,12},{12,8},{1,5},{5,1},{9,13},{13,9},{2,6},{6,2},{1... | collective-permute-start | bytes 196616 | tf_op jit(solution)/shard_map/ppermute | solution.py:25
  43.8 5.5 %collective-permute-start.9 = (bf16[16,2048]{1,0:T(8,128)(2,1)S(1)}, bf16[16,2048]{1,0:T(8,128)(2,1)S(1)}, u32[]{:S(2)}, u32[]{:S(2)}) collective-permute-start(bf16[16,2048]{1,0:T(8,128)(2,1)S(1)} %get-tuple-element.49), channel_id=1, source_target_pairs={{0,8},{4,12},{8,0},{12,4},{1,9},{5,13},{9,1},{13,5},{2,10},{6,14},... | collective-permute-start | bytes 196616 | tf_op jit(solution)/shard_map/ppermute | solution.py:25
